TPU v7x, 32 devices: a whole 2x2x4 slice. The times are simulated.
32 devices in a mesh: grp: 2 (over core), blk: 16 (over z, y, x).
Axes of the slice: x: 2, y: 2, z: 4, core: 2. Of those that a mesh axis runs over, the one named last changes fastest.
Arguments:
- factors: bfloat16 [128, 256, 512], P(('grp', 'blk')), may hold values from -6 to 6
- loadings: bfloat16 [512, 2048], replicated, may hold values from -0.25 to 0.25
- netload_map: bfloat16 [512, 200], replicated, may hold values from -0.25 to 0.25
- rule_weights: bfloat16 [16, 2048, 200], P('blk'), may hold values from -0.125 to 0.125
- rule_bias: float32 [16, 200], P('blk'), may hold values from -3 to 3
Outputs:
- decisions: bfloat16 [256, 128, 200], P('blk', 'grp')
- rule_grad: float32 [16, 2048, 200], P('blk', 'grp')
All inputs are finite; a program needn't handle non-finite values.
Results may differ from a plain program's by a relative error of at most 0.01.
Values may be sent and summed in bfloat16 or wider, within the bound.
No kernel may reach another device: no remote copies, remote signals or barrier semaphores. Data moves between devices by JAX's collectives and lax.ppermute only.
A program may use at most 128 MiB of HBM per device.

v0:
```python
import math

import jax
import jax.numpy as jnp
from jax import lax
from jax.sharding import PartitionSpec as P


def body(factors, loadings, netload_map, rule_weights, rule_bias):
    blocks = lax.axis_size("blk")
    groups = lax.axis_size("grp")
    path_dev, hours, width_k = factors.shape
    hour_blk = hours // blocks
    row_scale = 1.0 / math.sqrt(groups * blocks * path_dev * hour_blk)
    weights = rule_weights[0]
    offsets = rule_bias[0]
    ordered = jnp.transpose(factors.reshape(path_dev, blocks, hour_blk, width_k), (1, 2, 0, 3))
    shocks = lax.all_to_all(ordered, "blk", split_axis=0, concat_axis=2, tiled=True)[0]
    features = jnp.tanh(
        jnp.einsum("...c,cf->...f", shocks, loadings, preferred_element_type=jnp.float32)
    ).astype(jnp.bfloat16)
    net_load = jnp.einsum(
        "...c,cd->...d", shocks, netload_map, preferred_element_type=jnp.float32
    ).astype(jnp.bfloat16)
    dispatch = (
        jnp.einsum("krf,fd->krd", features, weights, preferred_element_type=jnp.float32) + offsets
    )
    shortfall = net_load.astype(jnp.float32) - dispatch
    slopes = (
        -4.0 * jax.nn.sigmoid(shortfall) + jax.nn.sigmoid(-shortfall) + 0.25 * dispatch
    ).astype(jnp.bfloat16)
    decisions, slopes, received = (dispatch.astype(jnp.bfloat16), slopes, features)
    partial_grad = (
        jnp.einsum("krf,krd->fd", received, slopes, preferred_element_type=jnp.float32) * row_scale
    )[None]
    summed = lax.psum(partial_grad.astype(jnp.bfloat16), "grp").astype(jnp.float32)
    owned = partial_grad.shape[1] // groups
    grad_share = lax.dynamic_slice_in_dim(summed, lax.axis_index("grp") * owned, owned, 1)
    return (decisions, grad_share)


def solution(mesh):
    return jax.shard_map(
        body,
        mesh=mesh,
        in_specs=(P(("grp", "blk"), None, None), P(), P(), P("blk", None, None), P("blk", None)),
        out_specs=(P("blk", "grp", None), P("blk", "grp", None)),
        check_vma=False,
    )
```

profile of v0, /device:TPU:0, one launch (start us, length us, event | category | flops | bytes accessed | tf_op | source)
XLA Modules:
  0.0 83.8 jit_solution(3170537584982653773)
XLA Ops:
  7.2 0.0 copy-start
  7.2 0.0 all-reduce.2.cloned.1.call-start
  7.2 2.2 %copy.8 = bf16[4,256,512]{2,0,1:T(4,128)(2,1)S(1)} copy(bf16[4,256,512]{2,1,0:T(8,128)(2,1)} %param.5) | data formatting | bytes 2097152 | tf_op args[0]
  9.4 34.5 %all_to_all.15 = bf16[16,16,4,512]{3,2,1,0:T(4,128)(2,1)S(1)} all-to-all(bf16[16,16,4,512]{3,2,1,0:T(4,128)(2,1)S(1)} %bitcast.35), channel_id=1, replica_groups=mesh['grp'=2,'blk'=16] {'blk'}, dimensions={0} | all-to-all | bytes 2097152 | tf_op jit(solution)/shard_map/all_to_all | solution.py:18
  43.9 0.5 copy.9
  44.4 1.1 %squeeze.6 = bf16[16,64,512]{2,1,0:T(8,128)(2,1)} reshape(bf16[1,16,16,4,512]{4,3,2,1,0:T(4,128)(2,1)S(1)} %copy.9) | data formatting | bytes 2097152 | tf_op jit(solution)/shard_map/squeeze | solution.py:18
  45.5 0.0 copy-done
  45.5 0.0 copy-start.2
  45.5 0.0 copy-start.4
  45.5 3.6 %tanh_convert_fusion = bf16[16,64,2048]{2,1,0:T(8,128)(2,1)S(1)} fusion(bf16[16,64,512]{2,1,0:T(8,128)(2,1)} %squeeze.6, bf16[512,2048]{1,0:T(8,128)(2,1)S(1)} %copy-done), kind=kOutput, calls=%fused_computation | convolution fusion | flops 2149580800 | bytes 7340032 | tf_op jit(solution)/shard_map/...c,cf->...f/dot_general | solution.py:20
  49.1 0.0 copy-start.5
  49.1 0.0 copy-start.1
  49.2 0.0 copy-start.3
  49.2 0.0 copy-done.2
  49.2 0.0 copy-done.4
  49.2 2.4 %fusion.15 = (bf16[16,64,200]{2,1,0:T(8,128)(2,1)}, f32[16,64,200]{2,1,0:T(8,128)}) fusion(f32[200]{0:T(256)S(1)} %bitcast.36, bf16[16,64,2048]{2,1,0:T(8,128)(2,1)S(1)} %tanh_convert_fusion, bf16[1,2048,200]{1,2,0:T(8,128)(2,1)S(1)} %copy-done.2), kind=kOutput, calls=%fused_computation.20 | convolution fusion | flops 839270400 | bytes 6243104 | tf_op jit(solution)/shard_map/krf,fd->krd/dot_general | solution.py:26
  51.6 0.0 copy-done.5
  51.6 0.0 copy-done.1
  51.6 0.0 copy-done.3
  51.6 5.6 %fusion.2 = bf16[1,2048,200]{1,2,0:T(8,128)(2,1)} fusion(bf16[16,64,2048]{2,1,0:T(8,128)(2,1)} %copy-done.5, f32[16,64,200]{2,1,0:T(8,128)} %get-tuple-element.3, bf16[16,64,512]{2,1,0:T(8,128)(2,1)S(1)} %copy-done.1, bf16[512,200]{0,1:T(8,128)(2,1)S(1)} %copy-done.3), kind=kOutput, calls=%fused_computation.4 | convolution fusion | flops 1052057600 | bytes 7086080 | tf_op jit(solution)/shard_map/krf,krd->fd/dot_general | solution.py:34
  57.2 0.0 all-reduce.2.cloned.1.call-update
  57.3 17.7 %all-reduce.2.cloned.1.call-done = bf16[1,2048,200]{1,2,0:T(8,128)(2,1)} async-done(((bf16[1,2048,200]{1,2,0:T(8,128)(2,1)}), bf16[1,2048,200]{1,2,0:T(8,128)(2,1)}) %all-reduce.2.cloned.1.call-update) | async-done | bytes 819216 | tf_op jit(solution)/shard_map/psum | solution.py:36
  75.0 2.0 %dynamic-slice_convert_fusion = f32[1,1024,200]{1,2,0:T(8,128)} fusion(bf16[1,2048,200]{1,2,0:T(8,128)(2,1)} %all-reduce.2.cloned.1.call-done, s32[]{:T(128)S(6)} %select_n.3), kind=kLoop, calls=%fused_computation.15 | loop fusion | flops 204800 | bytes 1228804 | tf_op jit(solution)/shard_map/convert_element_type | solution.py:36
Async XLA Ops:
  7.2 38.3 %copy-start = (bf16[512,2048]{1,0:T(8,128)(2,1)S(1)}, bf16[512,2048]{1,0:T(8,128)(2,1)}, u32[]{:S(2)}) copy-start(bf16[512,2048]{1,0:T(8,128)(2,1)} %param.6) | copy-start | bytes 6291460
  7.2 67.8 %all-reduce.2.cloned.1.call-start = ((), (), s32[]{:S(2)}) async-start(), calls=%async_computation.1 | async-start | bytes 1638400 | tf_op jit(solution)/shard_map/psum | solution.py:36
  45.5 3.7 %copy-start.2 = (bf16[1,2048,200]{1,2,0:T(8,128)(2,1)S(1)}, bf16[1,2048,200]{1,2,0:T(8,128)(2,1)}, u32[]{:S(2)}) copy-start(bf16[1,2048,200]{1,2,0:T(8,128)(2,1)} %param.8) | copy-start | bytes 2457604
  45.5 3.7 %copy-start.4 = (f32[1,200]{1,0:T(1,128)S(1)}, f32[1,200]{1,0:T(1,128)}, u32[]{:S(2)}) copy-start(f32[1,200]{1,0:T(1,128)} %param.9) | copy-start | bytes 2404
  49.1 2.5 %copy-start.5 = (bf16[16,64,2048]{2,1,0:T(8,128)(2,1)}, bf16[16,64,2048]{2,1,0:T(8,128)(2,1)S(1)}, u32[]{:S(2)}) copy-start(bf16[16,64,2048]{2,1,0:T(8,128)(2,1)S(1)} %tanh_convert_fusion) | copy-start | bytes 12582916
  49.1 2.5 %copy-start.1 = (bf16[16,64,512]{2,1,0:T(8,128)(2,1)S(1)}, bf16[16,64,512]{2,1,0:T(8,128)(2,1)}, u32[]{:S(2)}) copy-start(bf16[16,64,512]{2,1,0:T(8,128)(2,1)} %squeeze.6) | copy-start | bytes 3145732
  49.2 2.5 %copy-start.3 = (bf16[512,200]{0,1:T(8,128)(2,1)S(1)}, bf16[512,200]{0,1:T(8,128)(2,1)}, u32[]{:S(2)}) copy-start(bf16[512,200]{0,1:T(8,128)(2,1)} %param.7) | copy-start | bytes 614404
Sparse Core Ops, SparseCore 0:
  57.4 17.5 all-reduce.1
where the time goes:
time: 84 us; the launch traced here: 83.8 us
  blocking collectives  34.5 us (41%)
  waiting for transfers between devices  17.7 us (21%)
  between operations  14.1 us (17%)
  matrix products  11.7 us (14%)
  local copies, waits for them, and re-layouts  3.8 us (5%)
  other arithmetic  1.98 us (2%)
    all_to_all x1, blocking collectives, body(): lax.all_to_all(ordered, 'blk', split_axis=0, concat_axis=2, tiled=True)[0]  34.5 us
    psum x1, waiting for transfers between devices, body(): lax.psum(partial_grad.astype(jnp.bfloat16), 'grp').astype(jnp.float32)  17.7 us
    dot_general x1, matrix products, body(): jnp.einsum('krf,krd->fd', received, slopes, preferred_element_type=jnp.fl...  5.61 us
    dot_general x1, matrix products, body(): jnp.einsum('...c,cf->...f', shocks, loadings, preferred_element_type=jnp....  3.63 us
    dot_general x1, matrix products, body(): jnp.einsum('krf,fd->krd', features, weights, preferred_element_type=jnp.f...  2.44 us
    unnamed x13, local copies, waits for them, and re-layouts  2.21 us
    convert_element_type x1, other arithmetic, body(): lax.psum(partial_grad.astype(jnp.bfloat16), 'grp').astype(jnp.float32)  1.98 us
  transfers between devices with their start and end apart: 1, of which 1 were waited for; matrix products, arithmetic and copies ran while one was open for 0% of the time, Pallas kernels for 0%

commit v1 on v0

v1 whole, which is shorter than its diff:
```python
import functools
import math

import jax
import jax.numpy as jnp
from jax import lax
from jax.experimental import pallas as pl
from jax.experimental.pallas import tpu as pltpu
from jax.sharding import PartitionSpec as P

F32 = jnp.float32
BF16 = jnp.bfloat16
LANES = 128


def dot(a, b, ca, cb):
    return lax.dot_general(a, b, (((ca,), (cb,)), ((), ())), preferred_element_type=F32)


def block_of(size, target):
    while size % target:
        target //= 2
    return target


def rule_kernel(
    groups, hour_blk, row_scale,
    x_ref, load_ref, net_ref, weight_ref, bias_ref,
    dec_ref, send_ref, own_ref,
    feat, slope, disp,
):
    rows, width_f = feat.shape
    regions = weight_ref.shape[0]
    share = width_f // groups
    paths = rows // hour_blk
    row_step = block_of(rows, 256)
    feat_step = block_of(width_f, 512)
    cuts = [(c, min(LANES, regions - c)) for c in range(0, regions, LANES)]
    for r in range(0, rows, row_step):
        here = pl.ds(r, row_step)
        x = x_ref[here, :]
        for c in range(0, width_f, feat_step):
            z = jnp.dot(x, load_ref[:, pl.ds(c, feat_step)], preferred_element_type=F32)
            feat[here, pl.ds(c, feat_step)] = jnp.tanh(z).astype(BF16)
        net = dot(x, net_ref[...], 1, 1).astype(BF16).astype(F32)
        d = dot(feat[here, :], weight_ref[...], 1, 1) + bias_ref[...]
        for i, (c, w) in enumerate(cuts):
            disp[i, here, pl.ds(0, w)] = d[:, c : c + w]
        slope[here, :] = (-1.5 - 2.5 * jnp.tanh(0.5 * (net - d)) + 0.25 * d).astype(BF16)
    for h in range(hour_blk):
        for i, (c, w) in enumerate(cuts):
            dec_ref[h, :, pl.ds(c, w)] = disp[i, pl.ds(h, paths, stride=hour_blk), :][:, :w].astype(BF16)
    mine = lax.axis_index("grp")
    s = slope[...]
    grad_step = block_of(share, 512)
    for step in range(1, groups + 1):
        owner = lax.rem(mine + step, groups)
        for c in range(0, share, grad_step):
            at = pl.ds(pl.multiple_of(owner * share + c, LANES), grad_step)
            g = dot(s, feat[:, at], 0, 0) * row_scale
            if step < groups:
                send_ref[step - 1, :, pl.ds(c, grad_step)] = g.astype(BF16)
            else:
                own_ref[:, pl.ds(c, grad_step)] = g


def body(factors, loadings, netload_map, rule_weights, rule_bias):
    blocks = lax.axis_size("blk")
    groups = lax.axis_size("grp")
    path_dev, hours, width_k = factors.shape
    width_f = loadings.shape[1]
    regions = netload_map.shape[1]
    hour_blk = hours // blocks
    paths = path_dev * blocks
    rows = paths * hour_blk
    share = width_f // groups
    row_scale = 1.0 / math.sqrt(groups * rows)
    ordered = factors.reshape(path_dev, blocks, hour_blk, width_k).swapaxes(0, 1)
    ordered = ordered.reshape(blocks, path_dev * hour_blk, width_k)
    shocks = lax.all_to_all(ordered, "blk", split_axis=0, concat_axis=0, tiled=True)
    vmem = pl.BlockSpec(memory_space=pltpu.VMEM)
    decisions, send, own = pl.pallas_call(
        functools.partial(rule_kernel, groups, hour_blk, row_scale),
        out_shape=(
            jax.ShapeDtypeStruct((hour_blk, paths, regions), BF16),
            jax.ShapeDtypeStruct((max(groups - 1, 1), regions, share), BF16),
            jax.ShapeDtypeStruct((regions, share), F32),
        ),
        in_specs=[vmem] * 5,
        out_specs=[vmem] * 3,
        scratch_shapes=[
            pltpu.VMEM((rows, width_f), BF16),
            pltpu.VMEM((rows, regions), BF16),
            pltpu.VMEM((pl.cdiv(regions, LANES), rows, LANES), F32),
        ],
        compiler_params=pltpu.CompilerParams(vmem_limit_bytes=40 << 20),
        name="rules",
    )(
        shocks.reshape(rows, width_k),
        loadings,
        netload_map.T,
        rule_weights[0].T,
        rule_bias,
    )
    grad = own
    for step in range(1, groups):
        pairs = [(g, (g + step) % groups) for g in range(groups)]
        grad = grad + lax.ppermute(send[step - 1], "grp", pairs).astype(F32)
    return decisions, grad.T[None]


def solution(mesh):
    return jax.shard_map(
        body,
        mesh=mesh,
        in_specs=(P(("grp", "blk"), None, None), P(), P(), P("blk", None, None), P("blk", None)),
        out_specs=(P("blk", "grp", None), P("blk", "grp", None)),
        check_vma=False,
    )
```

time: 84 us -> 45.8 us (0.55)
  waiting for transfers between devices: 17.7 us -> 1.74 us
  between operations: 14.1 us -> 0.68 us
  matrix products: 11.7 us -> 0 us
  Pallas kernels: 0 us -> 6.2 us
  local copies, waits for them, and re-layouts: 3.8 us -> 1.48 us
  other arithmetic: 1.98 us -> 1.02 us
    psum x1 -> x0, waiting for transfers between devices: 17.7 us -> none  [body(): lax.psum(partial_grad.astype(jnp.bfloat16), 'grp').astype(jnp.float32)]
    dot_general x3 -> x0, matrix products: 11.7 us -> none  [the longest x1 5.61 us: body(): jnp.einsum('krf,krd->fd', received, slopes, preferred_element_type=jnp.fl...]
    pallas_call x0 -> x1, Pallas kernels: none -> 6.2 us  [body(): pl.pallas_call(functools.partial(rule_kernel, groups, hour_blk, row_scale...]
    unnamed x13 -> x8, local copies, waits for them, and re-layouts: 2.21 us -> 0.02 us
    convert_element_type x1 -> x0, other arithmetic: 1.98 us -> none  [body(): lax.psum(partial_grad.astype(jnp.bfloat16), 'grp').astype(jnp.float32)]
    ppermute x0 -> x1, waiting for transfers between devices: none -> 1.74 us  [body(): grad = grad + lax.ppermute(send[step - 1], 'grp', pairs).astype(F32)]
    transpose x0 -> x1, local copies, waits for them, and re-layouts: none -> 1.46 us  [body(): factors.reshape(path_dev, blocks, hour_blk, width_k).swapaxes(0, 1)]
    squeeze x1 -> x0, local copies, waits for them, and re-layouts: 1.11 us -> none  [body(): lax.all_to_all(ordered, 'blk', split_axis=0, concat_axis=2, tiled=True)[0]]
where the time goes in v1:
time: 45.8 us; the launch traced here: 45.6 us
  blocking collectives  34.5 us (75%)
  Pallas kernels  6.2 us (14%)
  waiting for transfers between devices  1.74 us (4%)
  local copies, waits for them, and re-layouts  1.48 us (3%)
  other arithmetic  1.02 us (2%)
  between operations  0.68 us (1%)
    all_to_all x1, blocking collectives, body(): lax.all_to_all(ordered, 'blk', split_axis=0, concat_axis=0, tiled=True)  34.5 us
    pallas_call x1, Pallas kernels, body(): pl.pallas_call(functools.partial(rule_kernel, groups, hour_blk, row_scale...  6.2 us
    ppermute x1, waiting for transfers between devices, body(): grad = grad + lax.ppermute(send[step - 1], 'grp', pairs).astype(F32)  1.74 us
    transpose x1, local copies, waits for them, and re-layouts, body(): factors.reshape(path_dev, blocks, hour_blk, width_k).swapaxes(0, 1)  1.46 us
    broadcast_in_dim x1, other arithmetic, body(): return (decisions, grad.T[None])  1.02 us
  transfers between devices with their start and end apart: 1, of which 1 were waited for; matrix products, arithmetic and copies ran while one was open for 0% of the time, Pallas kernels for 0%

profile of v1, /device:TPU:0, one launch (start us, length us, event | category | flops | bytes accessed | tf_op | source)
XLA Modules:
  0.0 45.6 jit_solution(426190053947565572)
XLA Ops:
  0.6 0.0 copy-start
  0.6 0.0 copy-start.1
  0.7 0.0 copy-start.2
  0.7 0.0 copy-start.3
  0.7 1.5 %copy.7 = bf16[16,4,16,512]{3,2,1,0:T(8,128)(2,1)S(1)} copy(bf16[16,4,16,512]{3,2,0,1:T(8,128)(2,1)} %bitcast.19) | data formatting | bytes 2097152 | tf_op jit(solution)/shard_map/transpose | solution.py:78
  2.1 34.5 %all_to_all.5 = bf16[16,64,512]{2,1,0:T(8,128)(2,1)S(1)} all-to-all(bf16[16,64,512]{2,1,0:T(8,128)(2,1)S(1)} %bitcast.18), channel_id=1, replica_groups=mesh['grp'=2,'blk'=16] {'blk'}, dimensions={0} | all-to-all | bytes 2097152 | tf_op jit(solution)/shard_map/all_to_all | solution.py:80
  36.6 0.0 copy-done
  36.6 0.0 copy-done.1
  36.6 0.0 copy-done.2
  36.6 0.0 copy-done.3
  36.6 6.2 %rules.1 = (bf16[16,64,200]{2,1,0:T(8,128)(2,1)}, bf16[1,200,1024]{2,1,0:T(8,128)(2,1)S(1)}, f32[200,1024]{1,0:T(8,128)S(1)}) custom-call(bf16[1024,512]{1,0:T(8,128)(2,1)S(1)} %bitcast.14, bf16[512,2048]{1,0:T(8,128)(2,1)S(1)} %copy-done, bf16[200,512]{1,0:T(8,128)(2,1)S(1)} %bitcast.16, bf16[200,2048]{1,0:T(8,128)(2,1)S(1)} %bitcast.15, f32[1,200]{1,0:T(1,128)S(1)} %copy-done.3), custom_call_target="tpu_custom_call" | custom-call | tf_op jit(solution)/shard_map/rules/pallas_call | solution.py:82
  42.8 0.0 collective-permute-start
  42.8 1.7 %collective-permute-done = bf16[200,1024]{1,0:T(8,128)(2,1)S(1)} collective-permute-done((bf16[200,1024]{1,0:T(8,128)(2,1)S(1)}, bf16[200,1024]{1,0:T(8,128)(2,1)S(1)}, u32[]{:S(2)}, u32[]{:S(2)}) %collective-permute-start) | collective-permute-done | bytes 409632 | tf_op jit(solution)/shard_map/ppermute | solution.py:108
  44.6 1.0 %add_bitcast_fusion = f32[1,1024,200]{1,2,0:T(8,128)} fusion(f32[200,1024]{1,0:T(8,128)S(1)} %get-tuple-element.6, bf16[200,1024]{1,0:T(8,128)(2,1)S(1)} %collective-permute-done), kind=kLoop, calls=%fused_computation | loop fusion | flops 409600 | bytes 2048000 | tf_op jit(solution)/shard_map/broadcast_in_dim | solution.py:109
Async XLA Ops:
  0.6 36.0 %copy-start = (bf16[512,2048]{1,0:T(8,128)(2,1)S(1)}, bf16[512,2048]{1,0:T(8,128)(2,1)}, u32[]{:S(2)}) copy-start(bf16[512,2048]{1,0:T(8,128)(2,1)} %load_ref.1) | copy-start | bytes 6291460
  0.6 36.0 %copy-start.1 = (bf16[1,2048,200]{1,2,0:T(8,128)(2,1)S(1)}, bf16[1,2048,200]{1,2,0:T(8,128)(2,1)}, u32[]{:S(2)}) copy-start(bf16[1,2048,200]{1,2,0:T(8,128)(2,1)} %param.8) | copy-start | bytes 2457604
  0.7 36.0 %copy-start.2 = (bf16[512,200]{0,1:T(8,128)(2,1)S(1)}, bf16[512,200]{0,1:T(8,128)(2,1)}, u32[]{:S(2)}) copy-start(bf16[512,200]{0,1:T(8,128)(2,1)} %param.7) | copy-start | bytes 614404
  0.7 36.0 %copy-start.3 = (f32[1,200]{1,0:T(1,128)S(1)}, f32[1,200]{1,0:T(1,128)}, u32[]{:S(2)}) copy-start(f32[1,200]{1,0:T(1,128)} %bias_ref.1) | copy-start | bytes 2404
  42.8 1.7 %collective-permute-start = (bf16[200,1024]{1,0:T(8,128)(2,1)S(1)}, bf16[200,1024]{1,0:T(8,128)(2,1)S(1)}, u32[]{:S(2)}, u32[]{:S(2)}) collective-permute-start(bf16[200,1024]{1,0:T(8,128)(2,1)S(1)} %bitcast.17), channel_id=1, source_target_pairs={{0,16},{16,0},{1,17},{17,1},{2,18},{18,2},{3,19},{19,3},{4,20},{20... | collective-permute-start | bytes 1228808 | tf_op jit(solution)/shard_map/ppermute | solution.py:108

commit v2 on v0

v2 whole, which is shorter than its diff:
```python
import functools
import math

import jax
import jax.numpy as jnp
from jax import lax
from jax.experimental import pallas as pl
from jax.experimental.pallas import tpu as pltpu
from jax.sharding import PartitionSpec as P

F32 = jnp.float32
BF16 = jnp.bfloat16
LANES = 128
PLANE = 4


def dot(a, b, ca, cb):
    return lax.dot_general(a, b, (((ca,), (cb,)), ((), ())), preferred_element_type=F32)


def block_of(size, target):
    while size % target:
        target //= 2
    return target


def cuts_of(regions):
    return [(i, c, min(LANES, regions - c)) for i, c in enumerate(range(0, regions, LANES))]


def place_of_device():
    me = lax.axis_index("blk")
    return me // PLANE, me % PLANE


def run_copies(moves, sem):
    copies = [pltpu.make_async_copy(a, b, sem.at[i]) for i, (a, b) in enumerate(moves)]
    for c in copies:
        c.start()
    for c in copies:
        c.wait()


def units_of(slow, path_dev, n1):
    half = slow // 2
    counts = [path_dev if dz < half else path_dev - n1 for dz in range(slow)]
    return counts, [sum(counts[:dz]) for dz in range(slow)]


def pack_far_kernel(n1, x_ref, *refs):
    outs, sem = refs[:-1], refs[-1]
    z, _ = place_of_device()
    half = len(outs)
    run_copies([(x_ref.at[pl.ds(0, n1), z ^ (half + i)], out) for i, out in enumerate(outs)], sem)


def pack_near_kernel(n1, x_ref, after_ref, *refs):
    nears, sem = refs[:-1], refs[-1]
    z, f = place_of_device()
    path_dev, slow = x_ref.shape[:2]
    counts, offs = units_of(slow, path_dev, n1)
    run_copies(
        [
            (x_ref.at[pl.ds(path_dev - counts[dz], counts[dz]), z ^ dz, f ^ d], near.at[pl.ds(offs[dz], counts[dz])])
            for dz in range(slow) for d, near in enumerate(nears)
        ],
        sem,
    )


def turn_near_kernel(offs, *refs):
    nears, outs = refs[:PLANE], refs[PLANE:]
    for out, off in zip(outs, offs):
        for d, near in enumerate(nears):
            out[d] = near[pl.ds(off, out.shape[1])]


def turn_far_kernel(half, *refs):
    fars, outs = refs[:half], refs[-PLANE:]
    _, f = place_of_device()
    for d, out in enumerate(outs):
        for i, far in enumerate(fars):
            out[i] = far[:, f ^ d]


def front(x, weights, feat, slope, at):
    load_ref, net_ref, weight_ref, bias_ref = weights
    here = pl.ds(at, x.shape[0])
    width_f = load_ref.shape[1]
    step = block_of(width_f, 512)
    for c in range(0, width_f, step):
        y = jnp.dot(x, load_ref[:, pl.ds(c, step)], preferred_element_type=F32)
        feat[here, pl.ds(c, step)] = jnp.tanh(y).astype(BF16)
    net = dot(x, net_ref[...], 1, 1).astype(BF16).astype(F32)
    d = dot(feat[here, :], weight_ref[...], 1, 1) + bias_ref[...]
    slope[here, :] = (-1.5 - 2.5 * jnp.tanh(0.5 * (net - d)) + 0.25 * d).astype(BF16)
    return d


def rules(pieces, path_dev, weights, disp_ref, feat, slope):
    z, f = place_of_device()
    at = 0
    while pieces:
        batch, size = [], 0
        while pieces and (not batch or size + math.prod(pieces[0][0].shape[:2]) <= 256):
            batch.append(pieces[0])
            size += math.prod(pieces[0][0].shape[:2])
            pieces = pieces[1:]
        x = jnp.concatenate([r[...].reshape(-1, r.shape[-1]) for r, _, _, _ in batch], 0)
        d = front(x, weights, feat, slope, at)
        row = 0
        for r, first, dz, df in batch:
            n, hour_blk = r.shape[:2]
            source = (z ^ dz) * PLANE + (f ^ df)
            start = pl.multiple_of((source * path_dev + first) * hour_blk, 16)
            for i, c, w in cuts_of(d.shape[1]):
                disp_ref[i, pl.ds(start, n * hour_blk), pl.ds(0, w)] = d[row : row + n * hour_blk, c : c + w]
            row += n * hour_blk
        at += size


def grad_parts(groups, slope, feat, steps):
    share = feat.shape[1] // groups
    mine = lax.axis_index("grp")
    s = slope[...]
    width = block_of(share, 512)
    for step in steps:
        owner = lax.rem(mine + step, groups)
        for c in range(0, share, width):
            at = pl.ds(pl.multiple_of(owner * share + c, LANES), width)
            yield step - 1, pl.ds(c, width), dot(s, feat[:, at], 0, 0)


def near_pieces(nears, path_dev):
    return [(near.at[pl.ds(0, path_dev)], 0, 0, d) for d, near in enumerate(nears)]


def plane_pieces(planes, dzs, first):
    return [(plane.at[d], first, dz, d) for plane, dz in zip(planes, dzs) for d in range(PLANE)]


def far_pieces(fars, half):
    return [(far.at[i], 0, half + i, d) for d, far in enumerate(fars) for i in range(half)]


def first_kernel(groups, path_dev, *refs):
    nears, weights, (disp_ref, acc_ref, slope, feat) = refs[:PLANE], refs[PLANE : PLANE + 4], refs[PLANE + 4 :]
    rules(near_pieces(nears, path_dev), path_dev, weights, disp_ref, feat, slope)
    for i, at, g in grad_parts(groups, slope, feat, range(1, groups + 1)):
        acc_ref[i, :, at] = g


def middle_kernel(groups, path_dev, half, *refs):
    k = half - 1
    planes, fars, refs = refs[:k], refs[k : k + PLANE], refs[k + PLANE :]
    weights, (disp_in, acc_in, disp_ref, acc_ref, slope, feat) = refs[:4], refs[4:]
    pieces = plane_pieces(planes, range(1, half), 0) + far_pieces(fars, half)
    rules(pieces, path_dev, weights, disp_ref, feat, slope)
    for i, at, g in grad_parts(groups, slope, feat, range(1, groups + 1)):
        acc_ref[i, :, at] = g + acc_in[i, :, at]


def last_kernel(groups, path_dev, half, n1, row_scale, *refs):
    planes, weights, refs = refs[:half], refs[half : half + 4], refs[half + 4 :]
    disp_in, acc_ref, disp_ref, send_ref, own_feat, slope, feat = refs
    rules(plane_pieces(planes, range(half, 2 * half), n1), path_dev, weights, disp_ref, feat, slope)
    for i, at, g in grad_parts(groups, slope, feat, range(1, groups)):
        send_ref[i, :, at] = ((g + acc_ref[i, :, at]) * row_scale).astype(BF16)
    share = own_feat.shape[1]
    own_feat[...] = feat[:, pl.ds(pl.multiple_of(lax.axis_index("grp") * share, LANES), share)]


def finish_kernel(row_scale, own_feat, slope, acc_ref, disp_ref, dec_ref, own_ref):
    last = acc_ref.shape[0] - 1
    share = own_feat.shape[1]
    hour_blk, paths, regions = dec_ref.shape
    s = slope[...]
    width = block_of(share, 512)
    for c in range(0, share, width):
        at = pl.ds(c, width)
        own_ref[:, at] = (dot(s, own_feat[:, at], 0, 0) + acc_ref[last, :, at]) * row_scale
    for h in range(hour_blk):
        for i, c, w in cuts_of(regions):
            dec_ref[h, :, pl.ds(c, w)] = disp_ref[i, pl.ds(h, paths, stride=hour_blk), :][:, :w].astype(BF16)


def call(kernel, name, outs, operands, scratch=(), flops=0, aliases=None, in_hbm=0):
    vmem = pl.BlockSpec(memory_space=pltpu.VMEM)
    hbm = pl.BlockSpec(memory_space=pl.ANY)
    moved = sum(math.prod(a.shape) * a.dtype.itemsize for a in [*operands, *outs])
    return pl.pallas_call(
        kernel,
        out_shape=tuple(outs),
        in_specs=[hbm] * in_hbm + [vmem] * (len(operands) - in_hbm),
        out_specs=[vmem] * len(outs),
        scratch_shapes=list(scratch),
        input_output_aliases=aliases or {},
        compiler_params=pltpu.CompilerParams(vmem_limit_bytes=16 << 20),
        cost_estimate=pl.CostEstimate(flops=0, bytes_accessed=0, transcendentals=0),
        name=name,
    )(*operands)


def body(factors, loadings, netload_map, rule_weights, rule_bias):
    blocks = lax.axis_size("blk")
    groups = lax.axis_size("grp")
    path_dev, hours, width_k = factors.shape
    width_f = loadings.shape[1]
    regions = netload_map.shape[1]
    hour_blk = hours // blocks
    paths = path_dev * blocks
    rows = paths * hour_blk
    share = width_f // groups
    slow = blocks // PLANE
    half = slow // 2
    row_scale = 1.0 / math.sqrt(groups * rows)
    n1 = path_dev // 2
    n2 = path_dev - n1
    counts, offs = units_of(slow, path_dev, n1)

    def hop(x, distance):
        return lax.ppermute(x, "blk", [(i, i ^ distance) for i in range(blocks)])

    def bf(*shape):
        return jax.ShapeDtypeStruct(shape, BF16)

    def f32(*shape):
        return jax.ShapeDtypeStruct(shape, F32)

    def sems(n):
        return [pltpu.SemaphoreType.DMA((n,))]

    view = factors.reshape(path_dev, slow, PLANE, hour_blk, width_k)
    fars = call(
        functools.partial(pack_far_kernel, n1), "pack_far",
        [bf(n1, PLANE, hour_blk, width_k)] * half, [view], sems(half), in_hbm=1,
    )
    nears = call(
        functools.partial(pack_near_kernel, n1), "pack_near",
        [bf(sum(counts), hour_blk, width_k)] * PLANE, [view, fars[0]], sems(slow * PLANE), in_hbm=2,
    )
    fars = [hop(x, (half + i) * PLANE) for i, x in enumerate(fars)]
    nears = [hop(x, d) if d else x for d, x in enumerate(nears)]
    planes = call(
        functools.partial(turn_near_kernel, offs[1:]), "turn_near",
        [bf(PLANE, counts[dz], hour_blk, width_k) for dz in range(1, slow)], nears,
    )
    fars = call(
        functools.partial(turn_far_kernel, half), "turn_far",
        [bf(half, n1, hour_blk, width_k)] * PLANE, fars,
    )
    planes = [hop(x, dz * PLANE) for dz, x in zip(range(1, slow), planes)]
    fars = [hop(x, d) if d else x for d, x in enumerate(fars)]

    weights = (loadings, netload_map.T, rule_weights[0].T, rule_bias)
    disp_shape = f32(pl.cdiv(regions, LANES), rows, LANES)
    acc_shape = f32(groups, regions, share)
    row_flops = 2.0 * (width_k * width_f + width_k * regions + 2 * width_f * regions)

    def scratch(n):
        return [pltpu.VMEM((n, regions), BF16), pltpu.VMEM((n, width_f), BF16)]

    n = PLANE * path_dev * hour_blk
    disp, acc = call(
        functools.partial(first_kernel, groups, path_dev), "rules_first",
        [disp_shape, acc_shape], [*nears, *weights], scratch(n), n * row_flops,
    )
    n = (half - 1) * PLANE * path_dev * hour_blk + half * PLANE * n1 * hour_blk
    k = half - 1 + PLANE + 4
    disp, acc = call(
        functools.partial(middle_kernel, groups, path_dev, half), "rules_middle",
        [disp_shape, acc_shape], [*planes[: half - 1], *fars, *weights, disp, acc],
        scratch(n), n * row_flops, {k: 0, k + 1: 1},
    )
    n = half * PLANE * n2 * hour_blk
    disp, send, own_feat, slope = call(
        functools.partial(last_kernel, groups, path_dev, half, n1, row_scale), "rules_last",
        [disp_shape, bf(max(groups - 1, 1), regions, share), bf(n, share), bf(n, regions)],
        [*planes[half - 1 :], *weights, disp, acc],
        [pltpu.VMEM((n, width_f), BF16)], n * row_flops, {half + 4: 0},
    )
    decisions, grad = call(
        functools.partial(finish_kernel, row_scale), "rules_finish",
        [bf(hour_blk, paths, regions), f32(regions, share)],
        [own_feat, slope, acc, disp], [], 2.0 * n * share * regions,
    )
    for step in range(1, groups):
        pairs = [(g, (g + step) % groups) for g in range(groups)]
        grad = grad + lax.ppermute(send[step - 1], "grp", pairs).astype(F32)
    return decisions, grad.T[None]


def solution(mesh):
    return jax.shard_map(
        body,
        mesh=mesh,
        in_specs=(P(("grp", "blk"), None, None), P(), P(), P("blk", None, None), P("blk", None)),
        out_specs=(P("blk", "grp", None), P("blk", "grp", None)),
        check_vma=False,
    )
```

time: 84 us -> 41 us (0.49)
  blocking collectives: 34.5 us -> 0 us
  starting transfers between devices: 0.04 us -> 18.9 us
  between operations: 14.1 us -> 0.72 us
  matrix products: 11.7 us -> 0 us
  Pallas kernels: 0 us -> 9.51 us
  waiting for transfers between devices: 17.7 us -> 9.47 us
  local copies, waits for them, and re-layouts: 3.8 us -> 1.23 us
  other arithmetic: 1.98 us -> 1.02 us
    all_to_all x1 -> x0, blocking collectives: 34.5 us -> none  [body(): lax.all_to_all(ordered, 'blk', split_axis=0, concat_axis=2, tiled=True)[0]]
    ppermute x0 -> x12, starting transfers between devices: none -> 18.9 us  [the longest x11 18.8 us: hop(): return lax.ppermute(x, 'blk', [(i, i ^ distance) for i in range(blocks)])]
    psum x1 -> x0, waiting for transfers between devices: 17.7 us -> none  [body(): lax.psum(partial_grad.astype(jnp.bfloat16), 'grp').astype(jnp.float32)]
    dot_general x3 -> x0, matrix products: 11.7 us -> none  [the longest x1 5.61 us: body(): jnp.einsum('krf,krd->fd', received, slopes, preferred_element_type=jnp.fl...]
    pallas_call x0 -> x8, Pallas kernels: none -> 9.51 us  [call(): pl.pallas_call(kernel, out_shape=tuple(outs), in_specs=[hbm] * in_hbm + [...]
    ppermute x0 -> x12, waiting for transfers between devices: none -> 9.47 us  [the longest x11 9.19 us: hop(): return lax.ppermute(x, 'blk', [(i, i ^ distance) for i in range(blocks)])]
    convert_element_type x1 -> x0, other arithmetic: 1.98 us -> none  [body(): lax.psum(partial_grad.astype(jnp.bfloat16), 'grp').astype(jnp.float32)]
    squeeze x1 -> x0, local copies, waits for them, and re-layouts: 1.11 us -> none  [body(): lax.all_to_all(ordered, 'blk', split_axis=0, concat_axis=2, tiled=True)[0]]
  transfers between devices with their start and end apart: 1 -> 12, of which waited for: 1 -> 5; matrix products, arithmetic and copies ran while one was open for 0% -> 0% of each run, Pallas kernels for 0% -> 17%
where the time goes in v2:
time: 41 us; the launch traced here: 40.8 us
  starting transfers between devices  18.9 us (46%)
  Pallas kernels  9.51 us (23%)
  waiting for transfers between devices  9.47 us (23%)
  local copies, waits for them, and re-layouts  1.23 us (3%)
  other arithmetic  1.02 us (2%)
  between operations  0.72 us (2%)
    ppermute x11, starting transfers between devices, hop(): return lax.ppermute(x, 'blk', [(i, i ^ distance) for i in range(blocks)])  18.8 us
    pallas_call x8, Pallas kernels, call(): pl.pallas_call(kernel, out_shape=tuple(outs), in_specs=[hbm] * in_hbm + [...  9.51 us
    ppermute x11, waiting for transfers between devices, hop(): return lax.ppermute(x, 'blk', [(i, i ^ distance) for i in range(blocks)])  9.19 us
    unnamed x10, local copies, waits for them, and re-layouts  1.23 us
    broadcast_in_dim x1, other arithmetic, body(): return (decisions, grad.T[None])  1.02 us
  transfers between devices with their start and end apart: 12, of which 5 were waited for; matrix products, arithmetic and copies ran while one was open for 0% of the time, Pallas kernels for 17%

profile of v2, /device:TPU:0, one launch (start us, length us, event | category | flops | bytes accessed | tf_op | source)
XLA Modules:
  0.0 40.8 jit_solution(10509080994598518073)
XLA Ops:
  0.6 1.2 %copy-done.2 = bf16[4,256,512]{2,1,0:T(8,128)(2,1)S(1)} copy-done((bf16[4,256,512]{2,1,0:T(8,128)(2,1)S(1)}, bf16[4,256,512]{2,1,0:T(8,128)(2,1)}, u32[]{:S(2)}) %copy-start.2) | copy-done | bytes 1048600
  1.9 0.2 pack_far.1
  2.1 0.5 %pack_near.1 = (bf16[12,16,512]{2,1,0:T(8,128)(2,1)S(1)}, bf16[12,16,512]{2,1,0:T(8,128)(2,1)S(1)}, bf16[12,16,512]{2,1,0:T(8,128)(2,1)S(1)}, bf16[12,16,512]{2,1,0:T(8,128)(2,1)S(1)}) custom-call(bf16[4,4,4,16,512]{4,3,2,1,0:T(8,128)(2,1)S(1)} %bitcast.14, bf16[2,4,16,512]{3,2,1,0:T(8,128)(2,1)S(1)} %get-tuple-element.25.after_ref), custom_call_target="tpu_custom_call" | custom-call | tf_op jit(solution)/shard_map/pack_near/pallas_call | solution.py:191
  2.6 3.0 %collective-permute-start = (bf16[12,16,512]{2,1,0:T(8,128)(2,1)S(1)}, bf16[12,16,512]{2,1,0:T(8,128)(2,1)S(1)}, u32[]{:S(2)}, u32[]{:S(2)}) collective-permute-start(bf16[12,16,512]{2,1,0:T(8,128)(2,1)S(1)} %get-tuple-element.27), channel_id=1, source_target_pairs={{0,1},{1,0},{2,3},{3,2},{4,5},{5,4},{6,7},{7,6},{8,9},{9,8},{10,11... | collective-permute-start | bytes 589832 | tf_op jit(solution)/shard_map/ppermute | solution.py:222
  5.6 1.5 %collective-permute-start.1 = (bf16[12,16,512]{2,1,0:T(8,128)(2,1)S(1)}, bf16[12,16,512]{2,1,0:T(8,128)(2,1)S(1)}, u32[]{:S(2)}, u32[]{:S(2)}) collective-permute-start(bf16[12,16,512]{2,1,0:T(8,128)(2,1)S(1)} %get-tuple-element.28), channel_id=1, source_target_pairs={{0,2},{1,3},{2,0},{3,1},{4,6},{5,7},{6,4},{7,5},{8,10},{9,11},{10,... | collective-permute-start | bytes 589832 | tf_op jit(solution)/shard_map/ppermute | solution.py:222
  7.2 3.0 %collective-permute-start.6 = (bf16[2,4,16,512]{3,2,1,0:T(8,128)(2,1)S(1)}, bf16[2,4,16,512]{3,2,1,0:T(8,128)(2,1)S(1)}, u32[]{:S(2)}, u32[]{:S(2)}) collective-permute-start(bf16[2,4,16,512]{3,2,1,0:T(8,128)(2,1)S(1)} %get-tuple-element.25.after_ref), channel_id=1, source_target_pairs={{0,8},{1,9},{2,10},{3,11},{4,12},{5,13},{6,14},{7,15},{8,0},{9,1},... | collective-permute-start | bytes 393224 | tf_op jit(solution)/shard_map/ppermute | solution.py:222
  10.2 1.3 %collective-permute-start.7 = (bf16[2,4,16,512]{3,2,1,0:T(8,128)(2,1)S(1)}, bf16[2,4,16,512]{3,2,1,0:T(8,128)(2,1)S(1)}, u32[]{:S(2)}, u32[]{:S(2)}) collective-permute-start(bf16[2,4,16,512]{3,2,1,0:T(8,128)(2,1)S(1)} %get-tuple-element.33), channel_id=1, source_target_pairs={{0,12},{1,13},{2,14},{3,15},{4,8},{5,9},{6,10},{7,11},{8,4},{9,5},... | collective-permute-start | bytes 393224 | tf_op jit(solution)/shard_map/ppermute | solution.py:222
  11.6 4.6 %collective-permute-done.1.refs_2_ = bf16[12,16,512]{2,1,0:T(8,128)(2,1)S(1)} collective-permute-done((bf16[12,16,512]{2,1,0:T(8,128)(2,1)S(1)}, bf16[12,16,512]{2,1,0:T(8,128)(2,1)S(1)}, u32[]{:S(2)}, u32[]{:S(2)}) %collective-permute-start.1) | collective-permute-done | bytes 196640 | tf_op jit(solution)/shard_map/ppermute | solution.py:222
  16.3 1.6 %collective-permute-start.5 = (bf16[4,4,16,512]{3,2,1,0:T(8,128)(2,1)S(1)}, bf16[4,4,16,512]{3,2,1,0:T(8,128)(2,1)S(1)}, u32[]{:S(2)}, u32[]{:S(2)}) collective-permute-start(bf16[4,4,16,512]{3,2,1,0:T(8,128)(2,1)S(1)} %get-tuple-element.32), channel_id=1, source_target_pairs={{0,4},{1,5},{2,6},{3,7},{4,0},{5,1},{6,2},{7,3},{8,12},{9,13},{10,... | collective-permute-start | bytes 786440 | tf_op jit(solution)/shard_map/ppermute | solution.py:222
  17.9 1.8 %collective-permute-done.6.refs_0_ = bf16[2,4,16,512]{3,2,1,0:T(8,128)(2,1)S(1)} collective-permute-done((bf16[2,4,16,512]{3,2,1,0:T(8,128)(2,1)S(1)}, bf16[2,4,16,512]{3,2,1,0:T(8,128)(2,1)S(1)}, u32[]{:S(2)}, u32[]{:S(2)}) %collective-permute-start.6) | collective-permute-done | bytes 131104 | tf_op jit(solution)/shard_map/ppermute | solution.py:222
  19.7 1.6 %collective-permute-start.8 = (bf16[2,2,16,512]{3,2,1,0:T(8,128)(2,1)S(1)}, bf16[2,2,16,512]{3,2,1,0:T(8,128)(2,1)S(1)}, u32[]{:S(2)}, u32[]{:S(2)}) collective-permute-start(bf16[2,2,16,512]{3,2,1,0:T(8,128)(2,1)S(1)} %get-tuple-element.35), channel_id=1, source_target_pairs={{0,1},{1,0},{2,3},{3,2},{4,5},{5,4},{6,7},{7,6},{8,9},{9,8},{10,11... | collective-permute-start | bytes 196616 | tf_op jit(solution)/shard_map/ppermute | solution.py:222
  21.3 4.2 %collective-permute-start.3 = (bf16[4,2,16,512]{3,2,1,0:T(8,128)(2,1)S(1)}, bf16[4,2,16,512]{3,2,1,0:T(8,128)(2,1)S(1)}, u32[]{:S(2)}, u32[]{:S(2)}) collective-permute-start(bf16[4,2,16,512]{3,2,1,0:T(8,128)(2,1)S(1)} %get-tuple-element.30), channel_id=1, source_target_pairs={{0,8},{1,9},{2,10},{3,11},{4,12},{5,13},{6,14},{7,15},{8,0},{9,1},... | collective-permute-start | bytes 393224 | tf_op jit(solution)/shard_map/ppermute | solution.py:222
  25.5 0.4 %collective-permute-start.4 = (bf16[4,2,16,512]{3,2,1,0:T(8,128)(2,1)S(1)}, bf16[4,2,16,512]{3,2,1,0:T(8,128)(2,1)S(1)}, u32[]{:S(2)}, u32[]{:S(2)}) collective-permute-start(bf16[4,2,16,512]{3,2,1,0:T(8,128)(2,1)S(1)} %get-tuple-element.31), channel_id=1, source_target_pairs={{0,12},{1,13},{2,14},{3,15},{4,8},{5,9},{6,10},{7,11},{8,4},{9,5},... | collective-permute-start | bytes 393224 | tf_op jit(solution)/shard_map/ppermute | solution.py:222
  26.0 1.5 %collective-permute-start.9 = (bf16[2,2,16,512]{3,2,1,0:T(8,128)(2,1)S(1)}, bf16[2,2,16,512]{3,2,1,0:T(8,128)(2,1)S(1)}, u32[]{:S(2)}, u32[]{:S(2)}) collective-permute-start(bf16[2,2,16,512]{3,2,1,0:T(8,128)(2,1)S(1)} %get-tuple-element.36), channel_id=1, source_target_pairs={{0,2},{1,3},{2,0},{3,1},{4,6},{5,7},{6,4},{7,5},{8,10},{9,11},{10,... | collective-permute-start | bytes 196616 | tf_op jit(solution)/shard_map/ppermute | solution.py:222
  27.5 0.5 %collective-permute-start.10 = (bf16[2,2,16,512]{3,2,1,0:T(8,128)(2,1)S(1)}, bf16[2,2,16,512]{3,2,1,0:T(8,128)(2,1)S(1)}, u32[]{:S(2)}, u32[]{:S(2)}) collective-permute-start(bf16[2,2,16,512]{3,2,1,0:T(8,128)(2,1)S(1)} %get-tuple-element.37), channel_id=1, source_target_pairs={{0,3},{1,2},{2,1},{3,0},{4,7},{5,6},{6,5},{7,4},{8,11},{9,10},{10,... | collective-permute-start | bytes 196616 | tf_op jit(solution)/shard_map/ppermute | solution.py:222
  28.0 2.0 %rules_first.1 = (f32[2,1024,128]{2,1,0:T(8,128)S(1)}, f32[2,200,1024]{2,1,0:T(8,128)S(1)}) custom-call(bf16[12,16,512]{2,1,0:T(8,128)(2,1)S(1)} %get-tuple-element.26.refs_0_, bf16[12,16,512]{2,1,0:T(8,128)(2,1)S(1)} %collective-permute-done.refs_1_, bf16[12,16,512]{2,1,0:T(8,128)(2,1)S(1)} %collective-permute-done.1.refs_2_, ...), custom_call_target="tpu_custom_call" | custom-call | tf_op jit(solution)/shard_map/rules_first/pallas_call | solution.py:191
  30.0 1.0 %collective-permute-done.9.refs_3_ = bf16[2,2,16,512]{3,2,1,0:T(8,128)(2,1)S(1)} collective-permute-done((bf16[2,2,16,512]{3,2,1,0:T(8,128)(2,1)S(1)}, bf16[2,2,16,512]{3,2,1,0:T(8,128)(2,1)S(1)}, u32[]{:S(2)}, u32[]{:S(2)}) %collective-permute-start.9) | collective-permute-done | bytes 65568 | tf_op jit(solution)/shard_map/ppermute | solution.py:222
  30.9 1.7 %collective-permute-done.10.refs_4_ = bf16[2,2,16,512]{3,2,1,0:T(8,128)(2,1)S(1)} collective-permute-done((bf16[2,2,16,512]{3,2,1,0:T(8,128)(2,1)S(1)}, bf16[2,2,16,512]{3,2,1,0:T(8,128)(2,1)S(1)}, u32[]{:S(2)}, u32[]{:S(2)}) %collective-permute-start.10) | collective-permute-done | bytes 65568 | tf_op jit(solution)/shard_map/ppermute | solution.py:222
  32.7 3.4 %rules_middle.1 = (f32[2,1024,128]{2,1,0:T(8,128)S(1)}, f32[2,200,1024]{2,1,0:T(8,128)S(1)}) custom-call(bf16[4,4,16,512]{3,2,1,0:T(8,128)(2,1)S(1)} %collective-permute-done.5.refs_0_, bf16[2,2,16,512]{3,2,1,0:T(8,128)(2,1)S(1)} %get-tuple-element.34.refs_1_, ...), custom_call_target="tpu_custom_call", output_to_operand_aliasing={{0}: (9, {}), {1}: (10, {})} | custom-call | tf_op jit(solution)/shard_map/rules_middle/pallas_call | solution.py:191
  36.2 1.8 %rules_last.1 = (f32[2,1024,128]{2,1,0:T(8,128)S(1)}, bf16[1,200,1024]{2,1,0:T(8,128)(2,1)S(1)}, bf16[256,1024]{1,0:T(8,128)(2,1)S(1)}, bf16[256,200]{1,0:T(8,128)(2,1)S(1)}) custom-call(bf16[4,2,16,512]{3,2,1,0:T(8,128)(2,1)S(1)} %collective-permute-done.3.refs_0_, ...), custom_call_target="tpu_custom_call", output_to_operand_aliasing={{0}: (6, {})} | custom-call | tf_op jit(solution)/shard_map/rules_last/pallas_call | solution.py:191
  38.0 0.1 collective-permute-start.11
  38.1 1.5 %rules_finish.1 = (bf16[16,64,200]{2,1,0:T(8,128)(2,1)}, f32[200,1024]{1,0:T(8,128)S(1)}) custom-call(bf16[256,1024]{1,0:T(8,128)(2,1)S(1)} %get-tuple-element.42.own_feat, bf16[256,200]{1,0:T(8,128)(2,1)S(1)} %get-tuple-element.43.slope, f32[2,200,1024]{2,1,0:T(8,128)S(1)} %get-tuple-element.41.refs_7_.acc_ref, f32[2,1024,128]{2,1,0:T(8,128)S(1)} %get-tuple-element.44.disp_ref), custom_call_target="tpu_custom_call" | custom-call | tf_op jit(solution)/shard_map/rules_finish/pallas_call | solution.py:191
  39.5 0.3 collective-permute-done.11
  39.8 1.0 %add_bitcast_fusion = f32[1,1024,200]{1,2,0:T(8,128)} fusion(f32[200,1024]{1,0:T(8,128)S(1)} %get-tuple-element.46, bf16[200,1024]{1,0:T(8,128)(2,1)S(1)} %collective-permute-done.11), kind=kLoop, calls=%fused_computation | loop fusion | flops 409600 | bytes 2048000 | tf_op jit(solution)/shard_map/broadcast_in_dim | solution.py:290
  (19 shorter events, 0.1 us)
Async XLA Ops:
  0.6 1.2 %copy-start.2 = (bf16[4,256,512]{2,1,0:T(8,128)(2,1)S(1)}, bf16[4,256,512]{2,1,0:T(8,128)(2,1)}, u32[]{:S(2)}) copy-start(bf16[4,256,512]{2,1,0:T(8,128)(2,1)} %param.5) | copy-start | bytes 3145732
  1.9 26.1 %copy-start = (bf16[512,2048]{1,0:T(8,128)(2,1)S(1)}, bf16[512,2048]{1,0:T(8,128)(2,1)}, u32[]{:S(2)}) copy-start(bf16[512,2048]{1,0:T(8,128)(2,1)} %refs_2_.1) | copy-start | bytes 6291460
  1.9 26.1 %copy-start.1 = (bf16[1,2048,200]{1,2,0:T(8,128)(2,1)S(1)}, bf16[1,2048,200]{1,2,0:T(8,128)(2,1)}, u32[]{:S(2)}) copy-start(bf16[1,2048,200]{1,2,0:T(8,128)(2,1)} %param.8) | copy-start | bytes 2457604
  1.9 26.1 %copy-start.3 = (bf16[512,200]{0,1:T(8,128)(2,1)S(1)}, bf16[512,200]{0,1:T(8,128)(2,1)}, u32[]{:S(2)}) copy-start(bf16[512,200]{0,1:T(8,128)(2,1)} %param.7) | copy-start | bytes 614404
  1.9 26.1 %copy-start.4 = (f32[1,200]{1,0:T(1,128)S(1)}, f32[1,200]{1,0:T(1,128)}, u32[]{:S(2)}) copy-start(f32[1,200]{1,0:T(1,128)} %refs_5_.3) | copy-start | bytes 2404
  2.6 8.9 %collective-permute-start = (bf16[12,16,512]{2,1,0:T(8,128)(2,1)S(1)}, bf16[12,16,512]{2,1,0:T(8,128)(2,1)S(1)}, u32[]{:S(2)}, u32[]{:S(2)}) collective-permute-start(bf16[12,16,512]{2,1,0:T(8,128)(2,1)S(1)} %get-tuple-element.27), channel_id=1, source_target_pairs={{0,1},{1,0},{2,3},{3,2},{4,5},{5,4},{6,7},{7,6},{8,9},{9,8},{10,11... | collective-permute-start | bytes 589832 | tf_op jit(solution)/shard_map/ppermute | solution.py:222
  5.6 10.6 %collective-permute-start.1 = (bf16[12,16,512]{2,1,0:T(8,128)(2,1)S(1)}, bf16[12,16,512]{2,1,0:T(8,128)(2,1)S(1)}, u32[]{:S(2)}, u32[]{:S(2)}) collective-permute-start(bf16[12,16,512]{2,1,0:T(8,128)(2,1)S(1)} %get-tuple-element.28), channel_id=1, source_target_pairs={{0,2},{1,3},{2,0},{3,1},{4,6},{5,7},{6,4},{7,5},{8,10},{9,11},{10,... | collective-permute-start | bytes 589832 | tf_op jit(solution)/shard_map/ppermute | solution.py:222
  7.2 9.1 %collective-permute-start.2 = (bf16[12,16,512]{2,1,0:T(8,128)(2,1)S(1)}, bf16[12,16,512]{2,1,0:T(8,128)(2,1)S(1)}, u32[]{:S(2)}, u32[]{:S(2)}) collective-permute-start(bf16[12,16,512]{2,1,0:T(8,128)(2,1)S(1)} %get-tuple-element.29), channel_id=1, source_target_pairs={{0,3},{1,2},{2,1},{3,0},{4,7},{5,6},{6,5},{7,4},{8,11},{9,10},{10,... | collective-permute-start | bytes 589832 | tf_op jit(solution)/shard_map/ppermute | solution.py:222
  7.2 12.5 %collective-permute-start.6 = (bf16[2,4,16,512]{3,2,1,0:T(8,128)(2,1)S(1)}, bf16[2,4,16,512]{3,2,1,0:T(8,128)(2,1)S(1)}, u32[]{:S(2)}, u32[]{:S(2)}) collective-permute-start(bf16[2,4,16,512]{3,2,1,0:T(8,128)(2,1)S(1)} %get-tuple-element.25.after_ref), channel_id=1, source_target_pairs={{0,8},{1,9},{2,10},{3,11},{4,12},{5,13},{6,14},{7,15},{8,0},{9,1},... | collective-permute-start | bytes 393224 | tf_op jit(solution)/shard_map/ppermute | solution.py:222
  10.2 7.7 %collective-permute-start.7 = (bf16[2,4,16,512]{3,2,1,0:T(8,128)(2,1)S(1)}, bf16[2,4,16,512]{3,2,1,0:T(8,128)(2,1)S(1)}, u32[]{:S(2)}, u32[]{:S(2)}) collective-permute-start(bf16[2,4,16,512]{3,2,1,0:T(8,128)(2,1)S(1)} %get-tuple-element.33), channel_id=1, source_target_pairs={{0,12},{1,13},{2,14},{3,15},{4,8},{5,9},{6,10},{7,11},{8,4},{9,5},... | collective-permute-start | bytes 393224 | tf_op jit(solution)/shard_map/ppermute | solution.py:222
  16.3 16.4 %collective-permute-start.5 = (bf16[4,4,16,512]{3,2,1,0:T(8,128)(2,1)S(1)}, bf16[4,4,16,512]{3,2,1,0:T(8,128)(2,1)S(1)}, u32[]{:S(2)}, u32[]{:S(2)}) collective-permute-start(bf16[4,4,16,512]{3,2,1,0:T(8,128)(2,1)S(1)} %get-tuple-element.32), channel_id=1, source_target_pairs={{0,4},{1,5},{2,6},{3,7},{4,0},{5,1},{6,2},{7,3},{8,12},{9,13},{10,... | collective-permute-start | bytes 786440 | tf_op jit(solution)/shard_map/ppermute | solution.py:222
  19.7 7.8 %collective-permute-start.8 = (bf16[2,2,16,512]{3,2,1,0:T(8,128)(2,1)S(1)}, bf16[2,2,16,512]{3,2,1,0:T(8,128)(2,1)S(1)}, u32[]{:S(2)}, u32[]{:S(2)}) collective-permute-start(bf16[2,2,16,512]{3,2,1,0:T(8,128)(2,1)S(1)} %get-tuple-element.35), channel_id=1, source_target_pairs={{0,1},{1,0},{2,3},{3,2},{4,5},{5,4},{6,7},{7,6},{8,9},{9,8},{10,11... | collective-permute-start | bytes 196616 | tf_op jit(solution)/shard_map/ppermute | solution.py:222
  21.3 14.8 %collective-permute-start.3 = (bf16[4,2,16,512]{3,2,1,0:T(8,128)(2,1)S(1)}, bf16[4,2,16,512]{3,2,1,0:T(8,128)(2,1)S(1)}, u32[]{:S(2)}, u32[]{:S(2)}) collective-permute-start(bf16[4,2,16,512]{3,2,1,0:T(8,128)(2,1)S(1)} %get-tuple-element.30), channel_id=1, source_target_pairs={{0,8},{1,9},{2,10},{3,11},{4,12},{5,13},{6,14},{7,15},{8,0},{9,1},... | collective-permute-start | bytes 393224 | tf_op jit(solution)/shard_map/ppermute | solution.py:222
  25.5 10.6 %collective-permute-start.4 = (bf16[4,2,16,512]{3,2,1,0:T(8,128)(2,1)S(1)}, bf16[4,2,16,512]{3,2,1,0:T(8,128)(2,1)S(1)}, u32[]{:S(2)}, u32[]{:S(2)}) collective-permute-start(bf16[4,2,16,512]{3,2,1,0:T(8,128)(2,1)S(1)} %get-tuple-element.31), channel_id=1, source_target_pairs={{0,12},{1,13},{2,14},{3,15},{4,8},{5,9},{6,10},{7,11},{8,4},{9,5},... | collective-permute-start | bytes 393224 | tf_op jit(solution)/shard_map/ppermute | solution.py:222
  26.0 5.0 %collective-permute-start.9 = (bf16[2,2,16,512]{3,2,1,0:T(8,128)(2,1)S(1)}, bf16[2,2,16,512]{3,2,1,0:T(8,128)(2,1)S(1)}, u32[]{:S(2)}, u32[]{:S(2)}) collective-permute-start(bf16[2,2,16,512]{3,2,1,0:T(8,128)(2,1)S(1)} %get-tuple-element.36), channel_id=1, source_target_pairs={{0,2},{1,3},{2,0},{3,1},{4,6},{5,7},{6,4},{7,5},{8,10},{9,11},{10,... | collective-permute-start | bytes 196616 | tf_op jit(solution)/shard_map/ppermute | solution.py:222
  27.5 5.2 %collective-permute-start.10 = (bf16[2,2,16,512]{3,2,1,0:T(8,128)(2,1)S(1)}, bf16[2,2,16,512]{3,2,1,0:T(8,128)(2,1)S(1)}, u32[]{:S(2)}, u32[]{:S(2)}) collective-permute-start(bf16[2,2,16,512]{3,2,1,0:T(8,128)(2,1)S(1)} %get-tuple-element.37), channel_id=1, source_target_pairs={{0,3},{1,2},{2,1},{3,0},{4,7},{5,6},{6,5},{7,4},{8,11},{9,10},{10,... | collective-permute-start | bytes 196616 | tf_op jit(solution)/shard_map/ppermute | solution.py:222
  38.0 1.8 %collective-permute-start.11 = (bf16[200,1024]{1,0:T(8,128)(2,1)S(1)}, bf16[200,1024]{1,0:T(8,128)(2,1)S(1)}, u32[]{:S(2)}, u32[]{:S(2)}) collective-permute-start(bf16[200,1024]{1,0:T(8,128)(2,1)S(1)} %bitcast.18), channel_id=1, source_target_pairs={{0,16},{16,0},{1,17},{17,1},{2,18},{18,2},{3,19},{19,3},{4,20},{20... | collective-permute-start | bytes 1228808 | tf_op jit(solution)/shard_map/ppermute | solution.py:289

commit v3 on v0

v3 whole, which is shorter than its diff:
```python
import functools
import math

import jax
import jax.numpy as jnp
from jax import lax
from jax.experimental import pallas as pl
from jax.experimental.pallas import tpu as pltpu
from jax.sharding import PartitionSpec as P

F32 = jnp.float32
BF16 = jnp.bfloat16
LANES = 128
PLANE = 4


def dot(a, b, ca, cb):
    return lax.dot_general(a, b, (((ca,), (cb,)), ((), ())), preferred_element_type=F32)


def block_of(size, target):
    while size % target:
        target //= 2
    return target


def cuts_of(regions):
    return [(i, c, min(LANES, regions - c)) for i, c in enumerate(range(0, regions, LANES))]


def run_copies(moves, sem):
    copies = [pltpu.make_async_copy(a, b, sem.at[i]) for i, (a, b) in enumerate(moves)]
    for c in copies:
        c.start()
    for c in copies:
        c.wait()


def flips(groups, blocks):
    return groups % 2 == 0 and blocks == PLANE * PLANE


def digits(cfg):
    groups, blocks = cfg
    me = lax.axis_index("blk")
    hi, lo = me // PLANE, me % PLANE
    if not flips(groups, blocks):
        return hi, lo, None
    flip = lax.axis_index("grp") % 2
    return jnp.where(flip, lo, hi), jnp.where(flip, hi, lo), flip


def block_id(a, b, flip):
    straight = a * PLANE + b
    return straight if flip is None else jnp.where(flip, b * PLANE + a, straight)


def far_first(k, radix):
    return radix - k if k else 0


def pack_kernel(cfg, x_ref, *outs):
    a, _, flip = digits(cfg)
    for k, out in enumerate(outs):
        for b in range(PLANE):
            out[b] = x_ref[:, block_id(a ^ far_first(k, len(outs)), b, flip)]


def front(x, weights, feat, slope, at):
    load_ref, net_ref, weight_ref, bias_ref = weights
    here = pl.ds(at, x.shape[0])
    width_f = load_ref.shape[1]
    step = block_of(width_f, 512)
    for c in range(0, width_f, step):
        y = jnp.dot(x, load_ref[:, pl.ds(c, step)], preferred_element_type=F32)
        feat[here, pl.ds(c, step)] = jnp.tanh(y).astype(BF16)
    net = dot(x, net_ref[...], 1, 1).astype(BF16).astype(F32)
    d = dot(feat[here, :], weight_ref[...], 1, 1) + bias_ref[...]
    slope[here, :] = (-1.5 - 2.5 * jnp.tanh(0.5 * (net - d)) + 0.25 * d).astype(BF16)
    return d


def rules(cfg, arrived, weights, disp_ref, feat, slope):
    a, b, flip = digits(cfg)
    radix = len(arrived[0][1])
    path_dev, hour_blk, width_k = arrived[0][1][0].shape
    piece = path_dev * hour_blk
    per = block_of(radix, max(256 // piece, 1))
    at = 0
    for m, parts in arrived:
        for k in range(0, radix, per):
            x = jnp.concatenate([p[...].reshape(piece, width_k) for p in parts[k : k + per]], 0)
            d = front(x, weights, feat, slope, at)
            for i in range(per):
                start = pl.multiple_of(block_id(a ^ far_first(k + i, radix), b ^ m, flip) * piece, 16)
                for j, c, w in cuts_of(d.shape[1]):
                    disp_ref[j, pl.ds(start, piece), pl.ds(0, w)] = d[i * piece : (i + 1) * piece, c : c + w]
            at += per * piece


def grad_parts(groups, slope, feat, steps):
    share = feat.shape[1] // groups
    mine = lax.axis_index("grp")
    s = slope[...]
    width = block_of(share, 512)
    for step in steps:
        owner = lax.rem(mine + step, groups)
        for c in range(0, share, width):
            at = pl.ds(pl.multiple_of(owner * share + c, LANES), width)
            yield step - 1, pl.ds(c, width), dot(s, feat[:, at], 0, 0)


def load_kernel(cfg, *refs):
    k = (len(refs) - 1) // 2
    _, _, flip = digits(cfg)

    def load():
        run_copies(list(zip(refs[:k], refs[k:-1])), refs[-1])

    if flip is None:
        load()
    else:
        pl.when(flip == 0)(load)


def own_digit(cfg, parts, weights, disp_ref, acc_ref, slope, feat):
    _, b, _ = digits(cfg)
    rules(cfg, [(0, [p.at[b] for p in parts])], weights, disp_ref, feat, slope)
    for i, at, g in grad_parts(cfg[0], slope, feat, range(1, cfg[0] + 1)):
        acc_ref[i, :, at] = g


def turn_kernel(cfg, radix, *refs):
    raw, refs = refs[:4], refs[4:]
    parts, refs = refs[:radix], refs[radix + 4 :]
    weights, outs, (disp_ref, acc_ref, slope, feat, sem) = refs[:4], refs[4:-5], refs[-5:]
    _, b, flip = digits(cfg)
    if flip is not None:
        @pl.when(flip == 1)
        def _():
            run_copies(list(zip(raw, weights)), sem)
            own_digit(cfg, parts, weights, disp_ref, acc_ref, slope, feat)
    for m, out in enumerate(outs, 1):
        for k, part in enumerate(parts):
            out[k] = part[b ^ m]


def first_kernel(cfg, radix, *refs):
    parts, weights, refs = refs[:radix], refs[radix : radix + 4], refs[radix + 4 :]
    disp_in, acc_in, disp_ref, acc_ref, slope, feat = refs
    _, _, flip = digits(cfg)
    if flip is None:
        own_digit(cfg, parts, weights, disp_ref, acc_ref, slope, feat)
    else:
        @pl.when(flip == 0)
        def _():
            own_digit(cfg, parts, weights, disp_ref, acc_ref, slope, feat)


def middle_kernel(cfg, ms, at, *refs):
    k = len(ms)
    xs, weights, refs = refs[:k], refs[k : k + 4], refs[k + 4 :]
    disp_ref, feat, slope = refs[-3:]
    rows = sum(math.prod(x.shape[:-1]) for x in xs)
    here = pl.ds(at, rows)
    rules(
        cfg, [(m, [x.at[i] for i in range(x.shape[0])]) for m, x in zip(ms, xs)], weights, disp_ref,
        feat.at[here], slope.at[here],
    )


def last_kernel(cfg, ms, at, row_scale, *refs):
    acc_ref, send_ref, refs = refs[0], refs[-4], refs[1:-4] + refs[-3:]
    middle_kernel(cfg, ms, at, *refs)
    _, feat, slope = refs[-3:]
    for i, cols, g in grad_parts(cfg[0], slope, feat, range(1, cfg[0])):
        send_ref[i, :, cols] = ((g + acc_ref[i, :, cols]) * row_scale).astype(BF16)


def finish_kernel(groups, row_scale, feat, slope, acc_ref, disp_ref, dec_ref, own_ref):
    hour_blk, paths, regions = dec_ref.shape
    for i, cols, g in grad_parts(groups, slope, feat, [groups]):
        own_ref[:, cols] = (g + acc_ref[i, :, cols]) * row_scale
    for h in range(hour_blk):
        for i, c, w in cuts_of(regions):
            dec_ref[h, :, pl.ds(c, w)] = disp_ref[i, pl.ds(h, paths, stride=hour_blk), :][:, :w].astype(BF16)


def call(kernel, name, outs, operands, scratch=(), aliases=None, in_hbm=0):
    vmem = pl.BlockSpec(memory_space=pltpu.VMEM)
    hbm = pl.BlockSpec(memory_space=pl.ANY)
    return pl.pallas_call(
        kernel,
        out_shape=tuple(outs),
        in_specs=[hbm] * in_hbm + [vmem] * (len(operands) - in_hbm),
        out_specs=[vmem] * len(outs),
        scratch_shapes=list(scratch),
        input_output_aliases=aliases or {},
        compiler_params=pltpu.CompilerParams(vmem_limit_bytes=16 << 20),
        cost_estimate=pl.CostEstimate(flops=0, bytes_accessed=0, transcendentals=0),
        name=name,
    )(*operands)


def body(factors, loadings, netload_map, rule_weights, rule_bias):
    blocks = lax.axis_size("blk")
    groups = lax.axis_size("grp")
    path_dev, hours, width_k = factors.shape
    width_f = loadings.shape[1]
    regions = netload_map.shape[1]
    hour_blk = hours // blocks
    paths = path_dev * blocks
    rows = paths * hour_blk
    share = width_f // groups
    radix = blocks // PLANE
    row_scale = 1.0 / math.sqrt(groups * rows)
    cfg = (groups, blocks)

    def bf(*shape):
        return jax.ShapeDtypeStruct(shape, BF16)

    def f32(*shape):
        return jax.ShapeDtypeStruct(shape, F32)

    def hop(x, straight, flipped):
        pairs = []
        for g in range(groups):
            distance = flipped if flips(groups, blocks) and g % 2 else straight
            pairs += [(g * blocks + i, g * blocks + (i ^ distance)) for i in range(blocks)]
        return lax.ppermute(x, ("grp", "blk"), pairs)

    parts = call(
        functools.partial(pack_kernel, cfg), "pack",
        [bf(PLANE, path_dev, hour_blk, width_k)] * radix,
        [factors.reshape(path_dev, blocks, hour_blk, width_k)],
    )
    dist = [far_first(k, radix) for k in range(radix)]
    parts = [hop(x, d * PLANE, d) if d else x for d, x in zip(dist, parts)]
    weights = (loadings, netload_map.T, rule_weights[0].T, rule_bias)
    raw = weights
    weights = call(
        functools.partial(load_kernel, cfg), "load", [jax.ShapeDtypeStruct(w.shape, w.dtype) for w in weights], weights,
        [pltpu.SemaphoreType.DMA((len(weights),))], in_hbm=len(weights),
    )
    disp_shape = f32(pl.cdiv(regions, LANES), rows, LANES)
    acc_shape = f32(groups, regions, share)

    def scratch(ms):
        n = len(ms) * rows // PLANE
        return [pltpu.VMEM((n, regions), BF16), pltpu.VMEM((n, width_f), BF16)]

    def inputs(ms):
        return [arrived[m] for m in ms]

    middle, last = [[1], [2]], [3]
    *turned, disp, acc = call(
        functools.partial(turn_kernel, cfg, radix), "turn",
        [jax.ShapeDtypeStruct(w.shape, w.dtype) for w in weights]
        + [bf(radix, path_dev, hour_blk, width_k)] * (PLANE - 1) + [disp_shape, acc_shape],
        [*raw, *parts, *weights], scratch([0]) + [pltpu.SemaphoreType.DMA((4,))],
        {4 + radix + i: i for i in range(4)}, in_hbm=4,
    )
    weights, turned = turned[:4], turned[4:]
    arrived = {m: hop(x, m, m * PLANE) for m, x in enumerate(turned, 1)}
    k = radix + 4
    disp, acc = call(
        functools.partial(first_kernel, cfg, radix), "rules_first",
        [disp_shape, acc_shape], [*parts, *weights, disp, acc], scratch([0]), {k: 0, k + 1: 1},
    )
    n = rows // PLANE
    late = (PLANE - 1) * n
    shapes = [disp_shape, bf(late, width_f), bf(late, regions)]
    state, at = [disp], 0
    for ms in middle:
        k = len(ms) + 4
        state = call(
            functools.partial(middle_kernel, cfg, ms, at), "rules_middle", shapes,
            [*inputs(ms), *weights, *state], aliases={k + i: i for i in range(len(state))},
        )
        at += len(ms) * n
    k = len(last) + 5
    send, disp, feat, slope = call(
        functools.partial(last_kernel, cfg, last, at, row_scale), "rules_last",
        [bf(max(groups - 1, 1), regions, share), *shapes],
        [acc, *inputs(last), *weights, *state], aliases={k + i: 1 + i for i in range(len(state))},
    )
    decisions, grad = call(
        functools.partial(finish_kernel, groups, row_scale), "rules_finish",
        [bf(hour_blk, paths, regions), f32(regions, share)], [feat, slope, acc, disp],
    )
    for step in range(1, groups):
        pairs = [(g, (g + step) % groups) for g in range(groups)]
        grad = grad + lax.ppermute(send[step - 1], "grp", pairs).astype(F32)
    return decisions, grad.T[None]


def solution(mesh):
    return jax.shard_map(
        body,
        mesh=mesh,
        in_specs=(P(("grp", "blk"), None, None), P(), P(), P("blk", None, None), P("blk", None)),
        out_specs=(P("blk", "grp", None), P("blk", "grp", None)),
        check_vma=False,
    )
```

time: 84 us -> 36.6 us (0.44)
  blocking collectives: 34.5 us -> 0 us
  between operations: 14.1 us -> 0.73 us
  matrix products: 11.7 us -> 0 us
  starting transfers between devices: 0.04 us -> 9.38 us
  Pallas kernels: 0 us -> 8.62 us
  waiting for transfers between devices: 17.7 us -> 10.9 us
  local copies, waits for them, and re-layouts: 3.8 us -> 5.64 us
  other arithmetic: 1.98 us -> 1.02 us
    all_to_all x1 -> x0, blocking collectives: 34.5 us -> none  [body(): lax.all_to_all(ordered, 'blk', split_axis=0, concat_axis=2, tiled=True)[0]]
    psum x1 -> x0, waiting for transfers between devices: 17.7 us -> none  [body(): lax.psum(partial_grad.astype(jnp.bfloat16), 'grp').astype(jnp.float32)]
    dot_general x3 -> x0, matrix products: 11.7 us -> none  [the longest x1 5.61 us: body(): jnp.einsum('krf,krd->fd', received, slopes, preferred_element_type=jnp.fl...]
    ppermute x0 -> x7, waiting for transfers between devices: none -> 10.9 us  [the longest x6 10.8 us: hop(): return lax.ppermute(x, ('grp', 'blk'), pairs)]
    ppermute x0 -> x7, starting transfers between devices: none -> 9.38 us  [the longest x6 9.31 us: hop(): return lax.ppermute(x, ('grp', 'blk'), pairs)]
    pallas_call x0 -> x8, Pallas kernels: none -> 8.62 us  [call(): pl.pallas_call(kernel, out_shape=tuple(outs), in_specs=[hbm] * in_hbm + [...]
    unnamed x13 -> x14, local copies, waits for them, and re-layouts: 2.21 us -> 5.64 us
    convert_element_type x1 -> x0, other arithmetic: 1.98 us -> none  [body(): lax.psum(partial_grad.astype(jnp.bfloat16), 'grp').astype(jnp.float32)]
  transfers between devices with their start and end apart: 1 -> 7, of which waited for: 1 -> 4; matrix products, arithmetic and copies ran while one was open for 0% -> 0% of each run, Pallas kernels for 0% -> 18%
where the time goes in v3:
time: 36.6 us; the launch traced here: 36.3 us
  waiting for transfers between devices  10.9 us (30%)
  starting transfers between devices  9.38 us (26%)
  Pallas kernels  8.62 us (24%)
  local copies, waits for them, and re-layouts  5.64 us (15%)
  other arithmetic  1.02 us (3%)
  between operations  0.73 us (2%)
    ppermute x6, waiting for transfers between devices, hop(): return lax.ppermute(x, ('grp', 'blk'), pairs)  10.8 us
    ppermute x6, starting transfers between devices, hop(): return lax.ppermute(x, ('grp', 'blk'), pairs)  9.31 us
    pallas_call x8, Pallas kernels, call(): pl.pallas_call(kernel, out_shape=tuple(outs), in_specs=[hbm] * in_hbm + [...  8.62 us
    unnamed x14, local copies, waits for them, and re-layouts  5.64 us
    broadcast_in_dim x1, other arithmetic, body(): return (decisions, grad.T[None])  1.02 us
  transfers between devices with their start and end apart: 7, of which 4 were waited for; matrix products, arithmetic and copies ran while one was open for 0% of the time, Pallas kernels for 18%

profile of v3, /device:TPU:0, one launch (start us, length us, event | category | flops | bytes accessed | tf_op | source)
XLA Modules:
  0.0 36.3 jit_solution(12005234910331323871)
XLA Ops:
  0.7 1.3 %copy-done.4 = bf16[4,256,512]{2,1,0:T(8,128)(2,1)S(1)} copy-done((bf16[4,256,512]{2,1,0:T(8,128)(2,1)S(1)}, bf16[4,256,512]{2,1,0:T(8,128)(2,1)}, u32[]{:S(2)}) %copy-start.4) | copy-done | bytes 1048600
  1.9 0.1 pack.1
  2.0 5.1 %collective-permute-start = (bf16[4,4,16,512]{3,2,1,0:T(8,128)(2,1)S(1)}, bf16[4,4,16,512]{3,2,1,0:T(8,128)(2,1)S(1)}, u32[]{:S(2)}, u32[]{:S(2)}) collective-permute-start(bf16[4,4,16,512]{3,2,1,0:T(8,128)(2,1)S(1)} %get-tuple-element.34), channel_id=1, source_target_pairs={{0,12},{1,13},{2,14},{3,15},{4,8},{5,9},{6,10},{7,11},{8,4},{9,5},... | collective-permute-start | bytes 786440 | tf_op jit(solution)/shard_map/ppermute | solution.py:230
  7.1 0.6 %collective-permute-start.2 = (bf16[4,4,16,512]{3,2,1,0:T(8,128)(2,1)S(1)}, bf16[4,4,16,512]{3,2,1,0:T(8,128)(2,1)S(1)}, u32[]{:S(2)}, u32[]{:S(2)}) collective-permute-start(bf16[4,4,16,512]{3,2,1,0:T(8,128)(2,1)S(1)} %get-tuple-element.36), channel_id=1, source_target_pairs={{0,4},{1,5},{2,6},{3,7},{4,0},{5,1},{6,2},{7,3},{8,12},{9,13},{10,... | collective-permute-start | bytes 786440 | tf_op jit(solution)/shard_map/ppermute | solution.py:230
  7.8 1.6 %copy-done = bf16[512,2048]{1,0:T(8,128)(2,1)S(1)} copy-done((bf16[512,2048]{1,0:T(8,128)(2,1)S(1)}, bf16[512,2048]{1,0:T(8,128)(2,1)}, u32[]{:S(2)}) %copy-start) | copy-done | bytes 2097176
  9.4 1.1 %copy-done.2 = bf16[1,2048,200]{1,2,0:T(8,128)(2,1)S(1)} copy-done((bf16[1,2048,200]{1,2,0:T(8,128)(2,1)S(1)}, bf16[1,2048,200]{1,2,0:T(8,128)(2,1)}, u32[]{:S(2)}) %copy-start.2) | copy-done | bytes 819224
  10.5 0.9 %copy-done.5 = bf16[512,200]{0,1:T(8,128)(2,1)S(1)} copy-done((bf16[512,200]{0,1:T(8,128)(2,1)S(1)}, bf16[512,200]{0,1:T(8,128)(2,1)}, u32[]{:S(2)}) %copy-start.5) | copy-done | bytes 204824
  11.4 0.7 %copy-done.6 = f32[1,200]{1,0:T(1,128)S(1)} copy-done((f32[1,200]{1,0:T(1,128)S(1)}, f32[1,200]{1,0:T(1,128)}, u32[]{:S(2)}) %copy-start.6) | copy-done | bytes 824
  12.1 0.5 %load.1 = (bf16[512,2048]{1,0:T(8,128)(2,1)S(1)}, bf16[200,512]{1,0:T(8,128)(2,1)S(1)}, bf16[200,2048]{1,0:T(8,128)(2,1)S(1)}, f32[1,200]{1,0:T(1,128)S(1)}) custom-call(bf16[512,2048]{1,0:T(8,128)(2,1)S(1)} %copy-done, bf16[200,512]{1,0:T(8,128)(2,1)S(1)} %bitcast.13, bf16[200,2048]{1,0:T(8,128)(2,1)S(1)} %bitcast.10, f32[1,200]{1,0:T(1,128)S(1)} %copy-done.6), custom_call_target="tpu_custom_call" | custom-call | tf_op jit(solution)/shard_map/load/pallas_call | solution.py:192
  12.7 6.8 %collective-permute-done.1.refs_6_.refs_2_ = bf16[4,4,16,512]{3,2,1,0:T(8,128)(2,1)S(1)} collective-permute-done((bf16[4,4,16,512]{3,2,1,0:T(8,128)(2,1)S(1)}, bf16[4,4,16,512]{3,2,1,0:T(8,128)(2,1)S(1)}, u32[]{:S(2)}, u32[]{:S(2)}) %collective-permute-start.1) | collective-permute-done | bytes 262176 | tf_op jit(solution)/shard_map/ppermute | solution.py:230
  19.5 0.1 turn.1
  19.6 1.6 %collective-permute-start.5 = (bf16[4,4,16,512]{3,2,1,0:T(8,128)(2,1)S(1)}, bf16[4,4,16,512]{3,2,1,0:T(8,128)(2,1)S(1)}, u32[]{:S(2)}, u32[]{:S(2)}) collective-permute-start(bf16[4,4,16,512]{3,2,1,0:T(8,128)(2,1)S(1)} %get-tuple-element.50), channel_id=1, source_target_pairs={{0,1},{1,0},{2,3},{3,2},{4,5},{5,4},{6,7},{7,6},{8,9},{9,8},{10,11... | collective-permute-start | bytes 786440 | tf_op jit(solution)/shard_map/ppermute | solution.py:230
  21.1 1.5 %collective-permute-start.4 = (bf16[4,4,16,512]{3,2,1,0:T(8,128)(2,1)S(1)}, bf16[4,4,16,512]{3,2,1,0:T(8,128)(2,1)S(1)}, u32[]{:S(2)}, u32[]{:S(2)}) collective-permute-start(bf16[4,4,16,512]{3,2,1,0:T(8,128)(2,1)S(1)} %get-tuple-element.49), channel_id=1, source_target_pairs={{0,2},{1,3},{2,0},{3,1},{4,6},{5,7},{6,4},{7,5},{8,10},{9,11},{10,... | collective-permute-start | bytes 786440 | tf_op jit(solution)/shard_map/ppermute | solution.py:230
  22.7 0.5 %collective-permute-start.3 = (bf16[4,4,16,512]{3,2,1,0:T(8,128)(2,1)S(1)}, bf16[4,4,16,512]{3,2,1,0:T(8,128)(2,1)S(1)}, u32[]{:S(2)}, u32[]{:S(2)}) collective-permute-start(bf16[4,4,16,512]{3,2,1,0:T(8,128)(2,1)S(1)} %get-tuple-element.48), channel_id=1, source_target_pairs={{0,3},{1,2},{2,1},{3,0},{4,7},{5,6},{6,5},{7,4},{8,11},{9,10},{10,... | collective-permute-start | bytes 786440 | tf_op jit(solution)/shard_map/ppermute | solution.py:230
  23.1 2.0 %rules_first.1 = (f32[2,1024,128]{2,1,0:T(8,128)S(1)}, f32[2,200,1024]{2,1,0:T(8,128)S(1)}) custom-call(bf16[4,4,16,512]{3,2,1,0:T(8,128)(2,1)S(1)} %get-tuple-element.33.refs_4_.refs_0_, bf16[4,4,16,512]{3,2,1,0:T(8,128)(2,1)S(1)} %collective-permute-done.refs_5_.refs_1_, ...), custom_call_target="tpu_custom_call", output_to_operand_aliasing={{0}: (8, {}), {1}: (9, {})} | custom-call | tf_op jit(solution)/shard_map/rules_first/pallas_call | solution.py:192
  25.1 0.9 %collective-permute-done.5.refs_0_ = bf16[4,4,16,512]{3,2,1,0:T(8,128)(2,1)S(1)} collective-permute-done((bf16[4,4,16,512]{3,2,1,0:T(8,128)(2,1)S(1)}, bf16[4,4,16,512]{3,2,1,0:T(8,128)(2,1)S(1)}, u32[]{:S(2)}, u32[]{:S(2)}) %collective-permute-start.5) | collective-permute-done | bytes 262176 | tf_op jit(solution)/shard_map/ppermute | solution.py:230
  26.0 1.1 %rules_middle.2 = (f32[2,1024,128]{2,1,0:T(8,128)S(1)}, bf16[768,2048]{1,0:T(8,128)(2,1)S(1)}, bf16[768,200]{1,0:T(8,128)(2,1)S(1)}) custom-call(bf16[4,4,16,512]{3,2,1,0:T(8,128)(2,1)S(1)} %collective-permute-done.5.refs_0_, bf16[512,2048]{1,0:T(8,128)(2,1)S(1)} %get-tuple-element.41.refs_4_.refs_1_.refs_2_, ...), custom_call_target="tpu_custom_call", output_to_operand_aliasing={{0}: (5, {})} | custom-call | tf_op jit(solution)/shard_map/rules_middle/pallas_call | solution.py:192
  27.2 3.2 %collective-permute-done.4.refs_0_ = bf16[4,4,16,512]{3,2,1,0:T(8,128)(2,1)S(1)} collective-permute-done((bf16[4,4,16,512]{3,2,1,0:T(8,128)(2,1)S(1)}, bf16[4,4,16,512]{3,2,1,0:T(8,128)(2,1)S(1)}, u32[]{:S(2)}, u32[]{:S(2)}) %collective-permute-start.4) | collective-permute-done | bytes 262176 | tf_op jit(solution)/shard_map/ppermute | solution.py:230
  30.3 1.1 %rules_middle.3 = (f32[2,1024,128]{2,1,0:T(8,128)S(1)}, bf16[768,2048]{1,0:T(8,128)(2,1)S(1)}, bf16[768,200]{1,0:T(8,128)(2,1)S(1)}) custom-call(bf16[4,4,16,512]{3,2,1,0:T(8,128)(2,1)S(1)} %collective-permute-done.4.refs_0_, ...), custom_call_target="tpu_custom_call", output_to_operand_aliasing={{0}: (5, {}), {1}: (6, {}), {2}: (7, {})} | custom-call | tf_op jit(solution)/shard_map/rules_middle/pallas_call | solution.py:192
  31.5 2.0 %rules_last.1 = (bf16[1,200,1024]{2,1,0:T(8,128)(2,1)S(1)}, f32[2,1024,128]{2,1,0:T(8,128)S(1)}, bf16[768,2048]{1,0:T(8,128)(2,1)S(1)}, bf16[768,200]{1,0:T(8,128)(2,1)S(1)}) custom-call(f32[2,200,1024]{2,1,0:T(8,128)S(1)} %get-tuple-element.47.refs_0_.acc_ref, ...), custom_call_target="tpu_custom_call", output_to_operand_aliasing={{1}: (6, {}), {2}: (7, {}), {3}: (8, {})} | custom-call | tf_op jit(solution)/shard_map/rules_last/pallas_call | solution.py:192
  33.5 0.1 collective-permute-start.6
  33.6 1.7 %rules_finish.1 = (bf16[16,64,200]{2,1,0:T(8,128)(2,1)}, f32[200,1024]{1,0:T(8,128)S(1)}) custom-call(bf16[768,2048]{1,0:T(8,128)(2,1)S(1)} %get-tuple-element.58.feat, bf16[768,200]{1,0:T(8,128)(2,1)S(1)} %get-tuple-element.59.slope, f32[2,200,1024]{2,1,0:T(8,128)S(1)} %get-tuple-element.47.refs_0_.acc_ref, f32[2,1024,128]{2,1,0:T(8,128)S(1)} %get-tuple-element.60.disp_ref), custom_call_target="tpu_custom_call" | custom-call | tf_op jit(solution)/shard_map/rules_finish/pallas_call | solution.py:192
  35.2 0.1 collective-permute-done.6
  35.3 1.0 %add_bitcast_fusion = f32[1,1024,200]{1,2,0:T(8,128)} fusion(f32[200,1024]{1,0:T(8,128)S(1)} %get-tuple-element.62, bf16[200,1024]{1,0:T(8,128)(2,1)S(1)} %collective-permute-done.6), kind=kLoop, calls=%fused_computation | loop fusion | flops 409600 | bytes 2048000 | tf_op jit(solution)/shard_map/broadcast_in_dim | solution.py:294
  (13 shorter events, 0.0 us)
Async XLA Ops:
  0.6 18.8 %copy-start.3 = (bf16[1,2048,200]{1,2,0:T(8,128)(2,1)S(1)}, bf16[1,2048,200]{1,2,0:T(8,128)(2,1)}, u32[]{:S(2)}) copy-start(bf16[1,2048,200]{1,2,0:T(8,128)(2,1)} %param.8) | copy-start | bytes 2457604
  0.6 1.3 %copy-start.4 = (bf16[4,256,512]{2,1,0:T(8,128)(2,1)S(1)}, bf16[4,256,512]{2,1,0:T(8,128)(2,1)}, u32[]{:S(2)}) copy-start(bf16[4,256,512]{2,1,0:T(8,128)(2,1)} %param.5) | copy-start | bytes 3145732
  2.0 10.7 %collective-permute-start = (bf16[4,4,16,512]{3,2,1,0:T(8,128)(2,1)S(1)}, bf16[4,4,16,512]{3,2,1,0:T(8,128)(2,1)S(1)}, u32[]{:S(2)}, u32[]{:S(2)}) collective-permute-start(bf16[4,4,16,512]{3,2,1,0:T(8,128)(2,1)S(1)} %get-tuple-element.34), channel_id=1, source_target_pairs={{0,12},{1,13},{2,14},{3,15},{4,8},{5,9},{6,10},{7,11},{8,4},{9,5},... | collective-permute-start | bytes 786440 | tf_op jit(solution)/shard_map/ppermute | solution.py:230
  7.1 12.3 %collective-permute-start.1 = (bf16[4,4,16,512]{3,2,1,0:T(8,128)(2,1)S(1)}, bf16[4,4,16,512]{3,2,1,0:T(8,128)(2,1)S(1)}, u32[]{:S(2)}, u32[]{:S(2)}) collective-permute-start(bf16[4,4,16,512]{3,2,1,0:T(8,128)(2,1)S(1)} %get-tuple-element.35), channel_id=1, source_target_pairs={{0,8},{1,9},{2,10},{3,11},{4,12},{5,13},{6,14},{7,15},{8,0},{9,1},... | collective-permute-start | bytes 786440 | tf_op jit(solution)/shard_map/ppermute | solution.py:230
  7.1 12.3 %collective-permute-start.2 = (bf16[4,4,16,512]{3,2,1,0:T(8,128)(2,1)S(1)}, bf16[4,4,16,512]{3,2,1,0:T(8,128)(2,1)S(1)}, u32[]{:S(2)}, u32[]{:S(2)}) collective-permute-start(bf16[4,4,16,512]{3,2,1,0:T(8,128)(2,1)S(1)} %get-tuple-element.36), channel_id=1, source_target_pairs={{0,4},{1,5},{2,6},{3,7},{4,0},{5,1},{6,2},{7,3},{8,12},{9,13},{10,... | collective-permute-start | bytes 786440 | tf_op jit(solution)/shard_map/ppermute | solution.py:230
  7.8 1.6 %copy-start = (bf16[512,2048]{1,0:T(8,128)(2,1)S(1)}, bf16[512,2048]{1,0:T(8,128)(2,1)}, u32[]{:S(2)}) copy-start(bf16[512,2048]{1,0:T(8,128)(2,1)} %refs_0_.3) | copy-start | bytes 6291460
  9.4 1.1 %copy-start.2 = (bf16[1,2048,200]{1,2,0:T(8,128)(2,1)S(1)}, bf16[1,2048,200]{1,2,0:T(8,128)(2,1)}, u32[]{:S(2)}) copy-start(bf16[1,2048,200]{1,2,0:T(8,128)(2,1)} %param.8) | copy-start | bytes 2457604
  10.5 0.9 %copy-start.5 = (bf16[512,200]{0,1:T(8,128)(2,1)S(1)}, bf16[512,200]{0,1:T(8,128)(2,1)}, u32[]{:S(2)}) copy-start(bf16[512,200]{0,1:T(8,128)(2,1)} %param.7) | copy-start | bytes 614404
  11.4 0.7 %copy-start.6 = (f32[1,200]{1,0:T(1,128)S(1)}, f32[1,200]{1,0:T(1,128)}, u32[]{:S(2)}) copy-start(f32[1,200]{1,0:T(1,128)} %refs_3_.3) | copy-start | bytes 2404
  12.1 7.3 %copy-start.1 = (bf16[512,2048]{1,0:T(8,128)(2,1)S(1)}, bf16[512,2048]{1,0:T(8,128)(2,1)}, u32[]{:S(2)}) copy-start(bf16[512,2048]{1,0:T(8,128)(2,1)} %refs_0_.3) | copy-start | bytes 6291460
  19.6 6.4 %collective-permute-start.5 = (bf16[4,4,16,512]{3,2,1,0:T(8,128)(2,1)S(1)}, bf16[4,4,16,512]{3,2,1,0:T(8,128)(2,1)S(1)}, u32[]{:S(2)}, u32[]{:S(2)}) collective-permute-start(bf16[4,4,16,512]{3,2,1,0:T(8,128)(2,1)S(1)} %get-tuple-element.50), channel_id=1, source_target_pairs={{0,1},{1,0},{2,3},{3,2},{4,5},{5,4},{6,7},{7,6},{8,9},{9,8},{10,11... | collective-permute-start | bytes 786440 | tf_op jit(solution)/shard_map/ppermute | solution.py:230
  21.1 9.2 %collective-permute-start.4 = (bf16[4,4,16,512]{3,2,1,0:T(8,128)(2,1)S(1)}, bf16[4,4,16,512]{3,2,1,0:T(8,128)(2,1)S(1)}, u32[]{:S(2)}, u32[]{:S(2)}) collective-permute-start(bf16[4,4,16,512]{3,2,1,0:T(8,128)(2,1)S(1)} %get-tuple-element.49), channel_id=1, source_target_pairs={{0,2},{1,3},{2,0},{3,1},{4,6},{5,7},{6,4},{7,5},{8,10},{9,11},{10,... | collective-permute-start | bytes 786440 | tf_op jit(solution)/shard_map/ppermute | solution.py:230
  22.7 8.8 %collective-permute-start.3 = (bf16[4,4,16,512]{3,2,1,0:T(8,128)(2,1)S(1)}, bf16[4,4,16,512]{3,2,1,0:T(8,128)(2,1)S(1)}, u32[]{:S(2)}, u32[]{:S(2)}) collective-permute-start(bf16[4,4,16,512]{3,2,1,0:T(8,128)(2,1)S(1)} %get-tuple-element.48), channel_id=1, source_target_pairs={{0,3},{1,2},{2,1},{3,0},{4,7},{5,6},{6,5},{7,4},{8,11},{9,10},{10,... | collective-permute-start | bytes 786440 | tf_op jit(solution)/shard_map/ppermute | solution.py:230
  33.5 1.8 %collective-permute-start.6 = (bf16[200,1024]{1,0:T(8,128)(2,1)S(1)}, bf16[200,1024]{1,0:T(8,128)(2,1)S(1)}, u32[]{:S(2)}, u32[]{:S(2)}) collective-permute-start(bf16[200,1024]{1,0:T(8,128)(2,1)S(1)} %bitcast.15), channel_id=1, source_target_pairs={{0,16},{16,0},{1,17},{17,1},{2,18},{18,2},{3,19},{19,3},{4,20},{20... | collective-permute-start | bytes 1228808 | tf_op jit(solution)/shard_map/ppermute | solution.py:293

commit v4 on v3

--- a/solution.py
+++ b/solution.py
@@ -55,15 +55,29 @@
     return straight if flip is None else jnp.where(flip, b * PLANE + a, straight)
 
 
-def far_first(k, radix):
-    return radix - k if k else 0
+FIRST_HOPS = (2, 1, 3)
+SECOND_HOPS = (2, 1, 3)
+FLIPPED_SECOND_HOPS = (1, 2, 3)
+
+
+def first_distance(k, radix):
+    if not k:
+        return 0
+    return FIRST_HOPS[k - 1] if radix == PLANE else radix - k
+
+
+def second_distance(m, flip):
+    if not m:
+        return 0
+    straight, flipped = SECOND_HOPS[m - 1], FLIPPED_SECOND_HOPS[m - 1]
+    return straight if flip is None else jnp.where(flip, flipped, straight)
 
 
 def pack_kernel(cfg, x_ref, *outs):
     a, _, flip = digits(cfg)
     for k, out in enumerate(outs):
         for b in range(PLANE):
-            out[b] = x_ref[:, block_id(a ^ far_first(k, len(outs)), b, flip)]
+            out[b] = x_ref[:, block_id(a ^ first_distance(k, len(outs)), b, flip)]
 
 
 def front(x, weights, feat, slope, at):
@@ -92,7 +106,7 @@
             x = jnp.concatenate([p[...].reshape(piece, width_k) for p in parts[k : k + per]], 0)
             d = front(x, weights, feat, slope, at)
             for i in range(per):
-                start = pl.multiple_of(block_id(a ^ far_first(k + i, radix), b ^ m, flip) * piece, 16)
+                start = pl.multiple_of(block_id(a ^ first_distance(k + i, radix), b ^ second_distance(m, flip), flip) * piece, 16)
                 for j, c, w in cuts_of(d.shape[1]):
                     disp_ref[j, pl.ds(start, piece), pl.ds(0, w)] = d[i * piece : (i + 1) * piece, c : c + w]
             at += per * piece
@@ -110,17 +124,9 @@
             yield step - 1, pl.ds(c, width), dot(s, feat[:, at], 0, 0)
 
 
-def load_kernel(cfg, *refs):
+def load_kernel(*refs):
     k = (len(refs) - 1) // 2
-    _, _, flip = digits(cfg)
-
-    def load():
-        run_copies(list(zip(refs[:k], refs[k:-1])), refs[-1])
-
-    if flip is None:
-        load()
-    else:
-        pl.when(flip == 0)(load)
+    run_copies(list(zip(refs[:k], refs[k:-1])), refs[-1])
 
 
 def own_digit(cfg, parts, weights, disp_ref, acc_ref, slope, feat):
@@ -131,18 +137,16 @@
 
 
 def turn_kernel(cfg, radix, *refs):
-    raw, refs = refs[:4], refs[4:]
-    parts, refs = refs[:radix], refs[radix + 4 :]
-    weights, outs, (disp_ref, acc_ref, slope, feat, sem) = refs[:4], refs[4:-5], refs[-5:]
+    parts, weights, refs = refs[:radix], refs[radix : radix + 4], refs[radix + 4 :]
+    outs, (disp_ref, acc_ref, slope, feat) = refs[:-4], refs[-4:]
     _, b, flip = digits(cfg)
     if flip is not None:
         @pl.when(flip == 1)
         def _():
-            run_copies(list(zip(raw, weights)), sem)
             own_digit(cfg, parts, weights, disp_ref, acc_ref, slope, feat)
     for m, out in enumerate(outs, 1):
         for k, part in enumerate(parts):
-            out[k] = part[b ^ m]
+            out[k] = part[b ^ second_distance(m, flip)]
 
 
 def first_kernel(cfg, radix, *refs):
@@ -155,6 +159,15 @@
         @pl.when(flip == 0)
         def _():
             own_digit(cfg, parts, weights, disp_ref, acc_ref, slope, feat)
+
+
+def gather_kernel(cfg, ms, *refs):
+    k = len(ms)
+    xs, weights, refs = refs[:k], refs[k : k + 4], refs[k + 4 :]
+    disp_in, acc_in, disp_ref, acc_ref, slope, feat = refs
+    rules(cfg, [(m, [x.at[i] for i in range(x.shape[0])]) for m, x in zip(ms, xs)], weights, disp_ref, feat, slope)
+    for i, cols, g in grad_parts(cfg[0], slope, feat, range(1, cfg[0] + 1)):
+        acc_ref[i, :, cols] = g + acc_in[i, :, cols]
 
 
 def middle_kernel(cfg, ms, at, *refs):
@@ -234,12 +247,11 @@
         [bf(PLANE, path_dev, hour_blk, width_k)] * radix,
         [factors.reshape(path_dev, blocks, hour_blk, width_k)],
     )
-    dist = [far_first(k, radix) for k in range(radix)]
+    dist = [first_distance(k, radix) for k in range(radix)]
     parts = [hop(x, d * PLANE, d) if d else x for d, x in zip(dist, parts)]
     weights = (loadings, netload_map.T, rule_weights[0].T, rule_bias)
-    raw = weights
     weights = call(
-        functools.partial(load_kernel, cfg), "load", [jax.ShapeDtypeStruct(w.shape, w.dtype) for w in weights], weights,
+        load_kernel, "load", [jax.ShapeDtypeStruct(w.shape, w.dtype) for w in weights], weights,
         [pltpu.SemaphoreType.DMA((len(weights),))], in_hbm=len(weights),
     )
     disp_shape = f32(pl.cdiv(regions, LANES), rows, LANES)
@@ -255,20 +267,23 @@
     middle, last = [[1], [2]], [3]
     *turned, disp, acc = call(
         functools.partial(turn_kernel, cfg, radix), "turn",
-        [jax.ShapeDtypeStruct(w.shape, w.dtype) for w in weights]
-        + [bf(radix, path_dev, hour_blk, width_k)] * (PLANE - 1) + [disp_shape, acc_shape],
-        [*raw, *parts, *weights], scratch([0]) + [pltpu.SemaphoreType.DMA((4,))],
-        {4 + radix + i: i for i in range(4)}, in_hbm=4,
-    )
-    weights, turned = turned[:4], turned[4:]
-    arrived = {m: hop(x, m, m * PLANE) for m, x in enumerate(turned, 1)}
+        [bf(radix, path_dev, hour_blk, width_k)] * (PLANE - 1) + [disp_shape, acc_shape],
+        [*parts, *weights], scratch([0]),
+    )
+    arrived = {m: hop(x, SECOND_HOPS[m - 1], FLIPPED_SECOND_HOPS[m - 1] * PLANE) for m, x in enumerate(turned, 1)}
     k = radix + 4
     disp, acc = call(
         functools.partial(first_kernel, cfg, radix), "rules_first",
         [disp_shape, acc_shape], [*parts, *weights, disp, acc], scratch([0]), {k: 0, k + 1: 1},
     )
     n = rows // PLANE
-    late = (PLANE - 1) * n
+    early, middle = middle[0], middle[1:]
+    late = (PLANE - 1 - len(early)) * n
+    k = len(early) + 4
+    disp, acc = call(
+        functools.partial(gather_kernel, cfg, early), "rules_gather", [disp_shape, acc_shape],
+        [*inputs(early), *weights, disp, acc], scratch(early), {k: 0, k + 1: 1},
+    )
     shapes = [disp_shape, bf(late, width_f), bf(late, regions)]
     state, at = [disp], 0
     for ms in middle:

time: 36.6 us -> 34.5 us (0.943)
  waiting for transfers between devices: 10.9 us -> 6.9 us
  starting transfers between devices: 9.38 us -> 10.4 us
  Pallas kernels: 8.62 us -> 9.35 us
    ppermute x6, waiting for transfers between devices: 10.8 us -> 6.9 us  [hop(): return lax.ppermute(x, ('grp', 'blk'), pairs)]
    ppermute x1, starting transfers between devices: 0.07 us -> 1.17 us  [body(): grad = grad + lax.ppermute(send[step - 1], 'grp', pairs).astype(F32)]
    pallas_call x8, Pallas kernels: 8.62 us -> 9.35 us  [call(): pl.pallas_call(kernel, out_shape=tuple(outs), in_specs=[hbm] * in_hbm + [...]
    unnamed x14 -> x10, local copies, waits for them, and re-layouts: 5.64 us -> 5.56 us
  transfers between devices with their start and end apart: 7 -> 7, of which waited for: 4 -> 5; matrix products, arithmetic and copies ran while one was open for 0% -> 0% of each run, Pallas kernels for 18% -> 22%
where the time goes in v4:
time: 34.5 us; the launch traced here: 33.9 us
  starting transfers between devices  10.4 us (30%)
  Pallas kernels  9.35 us (27%)
  waiting for transfers between devices  6.9 us (20%)
  local copies, waits for them, and re-layouts  5.56 us (16%)
  other arithmetic  1.02 us (3%)
  between operations  0.7 us (2%)
    pallas_call x8, Pallas kernels, call(): pl.pallas_call(kernel, out_shape=tuple(outs), in_specs=[hbm] * in_hbm + [...  9.35 us
    ppermute x6, starting transfers between devices, hop(): return lax.ppermute(x, ('grp', 'blk'), pairs)  9.23 us
    ppermute x6, waiting for transfers between devices, hop(): return lax.ppermute(x, ('grp', 'blk'), pairs)  6.9 us
    unnamed x10, local copies, waits for them, and re-layouts  5.56 us
    ppermute x1, starting transfers between devices, body(): grad = grad + lax.ppermute(send[step - 1], 'grp', pairs).astype(F32)  1.17 us
    broadcast_in_dim x1, other arithmetic, body(): return (decisions, grad.T[None])  1.02 us
  transfers between devices with their start and end apart: 7, of which 5 were waited for; matrix products, arithmetic and copies ran while one was open for 0% of the time, Pallas kernels for 22%

profile of v4, /device:TPU:0, one launch (start us, length us, event | category | flops | bytes accessed | tf_op | source)
XLA Modules:
  0.0 33.9 jit_solution(5127106740550180898)
XLA Ops:
  0.6 1.2 %copy-done.1 = bf16[4,256,512]{2,1,0:T(8,128)(2,1)S(1)} copy-done((bf16[4,256,512]{2,1,0:T(8,128)(2,1)S(1)}, bf16[4,256,512]{2,1,0:T(8,128)(2,1)}, u32[]{:S(2)}) %copy-start.1) | copy-done | bytes 1048600
  1.9 0.1 pack.1
  1.9 4.1 %collective-permute-start = (bf16[4,4,16,512]{3,2,1,0:T(8,128)(2,1)S(1)}, bf16[4,4,16,512]{3,2,1,0:T(8,128)(2,1)S(1)}, u32[]{:S(2)}, u32[]{:S(2)}) collective-permute-start(bf16[4,4,16,512]{3,2,1,0:T(8,128)(2,1)S(1)} %get-tuple-element.29), channel_id=1, source_target_pairs={{0,8},{1,9},{2,10},{3,11},{4,12},{5,13},{6,14},{7,15},{8,0},{9,1},... | collective-permute-start | bytes 786440 | tf_op jit(solution)/shard_map/ppermute | solution.py:243
  6.0 1.6 %collective-permute-start.1 = (bf16[4,4,16,512]{3,2,1,0:T(8,128)(2,1)S(1)}, bf16[4,4,16,512]{3,2,1,0:T(8,128)(2,1)S(1)}, u32[]{:S(2)}, u32[]{:S(2)}) collective-permute-start(bf16[4,4,16,512]{3,2,1,0:T(8,128)(2,1)S(1)} %get-tuple-element.30), channel_id=1, source_target_pairs={{0,4},{1,5},{2,6},{3,7},{4,0},{5,1},{6,2},{7,3},{8,12},{9,13},{10,... | collective-permute-start | bytes 786440 | tf_op jit(solution)/shard_map/ppermute | solution.py:243
  7.6 1.6 %copy-done = bf16[512,2048]{1,0:T(8,128)(2,1)S(1)} copy-done((bf16[512,2048]{1,0:T(8,128)(2,1)S(1)}, bf16[512,2048]{1,0:T(8,128)(2,1)}, u32[]{:S(2)}) %copy-start) | copy-done | bytes 2097176
  9.2 1.1 %copy-done.2 = bf16[1,2048,200]{1,2,0:T(8,128)(2,1)S(1)} copy-done((bf16[1,2048,200]{1,2,0:T(8,128)(2,1)S(1)}, bf16[1,2048,200]{1,2,0:T(8,128)(2,1)}, u32[]{:S(2)}) %copy-start.2) | copy-done | bytes 819224
  10.3 0.9 %copy-done.3 = bf16[512,200]{0,1:T(8,128)(2,1)S(1)} copy-done((bf16[512,200]{0,1:T(8,128)(2,1)S(1)}, bf16[512,200]{0,1:T(8,128)(2,1)}, u32[]{:S(2)}) %copy-start.3) | copy-done | bytes 204824
  11.3 0.7 %copy-done.4 = f32[1,200]{1,0:T(1,128)S(1)} copy-done((f32[1,200]{1,0:T(1,128)S(1)}, f32[1,200]{1,0:T(1,128)}, u32[]{:S(2)}) %copy-start.4) | copy-done | bytes 824
  12.0 0.5 %load.1 = (bf16[512,2048]{1,0:T(8,128)(2,1)S(1)}, bf16[200,512]{1,0:T(8,128)(2,1)S(1)}, bf16[200,2048]{1,0:T(8,128)(2,1)S(1)}, f32[1,200]{1,0:T(1,128)S(1)}) custom-call(bf16[512,2048]{1,0:T(8,128)(2,1)S(1)} %copy-done, bf16[200,512]{1,0:T(8,128)(2,1)S(1)} %bitcast.12, bf16[200,2048]{1,0:T(8,128)(2,1)S(1)} %bitcast.11, f32[1,200]{1,0:T(1,128)S(1)} %copy-done.4), custom_call_target="tpu_custom_call" | custom-call | tf_op jit(solution)/shard_map/load/pallas_call | solution.py:205
  12.5 0.8 %collective-permute-done.refs_1_ = bf16[4,4,16,512]{3,2,1,0:T(8,128)(2,1)S(1)} collective-permute-done((bf16[4,4,16,512]{3,2,1,0:T(8,128)(2,1)S(1)}, bf16[4,4,16,512]{3,2,1,0:T(8,128)(2,1)S(1)}, u32[]{:S(2)}, u32[]{:S(2)}) %collective-permute-start) | collective-permute-done | bytes 262176 | tf_op jit(solution)/shard_map/ppermute | solution.py:243
  13.3 0.5 %collective-permute-done.1.refs_2_ = bf16[4,4,16,512]{3,2,1,0:T(8,128)(2,1)S(1)} collective-permute-done((bf16[4,4,16,512]{3,2,1,0:T(8,128)(2,1)S(1)}, bf16[4,4,16,512]{3,2,1,0:T(8,128)(2,1)S(1)}, u32[]{:S(2)}, u32[]{:S(2)}) %collective-permute-start.1) | collective-permute-done | bytes 262176 | tf_op jit(solution)/shard_map/ppermute | solution.py:243
  13.8 3.7 %collective-permute-done.2.refs_3_ = bf16[4,4,16,512]{3,2,1,0:T(8,128)(2,1)S(1)} collective-permute-done((bf16[4,4,16,512]{3,2,1,0:T(8,128)(2,1)S(1)}, bf16[4,4,16,512]{3,2,1,0:T(8,128)(2,1)S(1)}, u32[]{:S(2)}, u32[]{:S(2)}) %collective-permute-start.2) | collective-permute-done | bytes 262176 | tf_op jit(solution)/shard_map/ppermute | solution.py:243
  17.6 1.6 %collective-permute-start.3 = (bf16[4,4,16,512]{3,2,1,0:T(8,128)(2,1)S(1)}, bf16[4,4,16,512]{3,2,1,0:T(8,128)(2,1)S(1)}, u32[]{:S(2)}, u32[]{:S(2)}) collective-permute-start(bf16[4,4,16,512]{3,2,1,0:T(8,128)(2,1)S(1)} %get-tuple-element.36), channel_id=1, source_target_pairs={{0,2},{1,3},{2,0},{3,1},{4,6},{5,7},{6,4},{7,5},{8,10},{9,11},{10,... | collective-permute-start | bytes 786440 | tf_op jit(solution)/shard_map/ppermute | solution.py:243
  19.1 1.5 %collective-permute-start.5 = (bf16[4,4,16,512]{3,2,1,0:T(8,128)(2,1)S(1)}, bf16[4,4,16,512]{3,2,1,0:T(8,128)(2,1)S(1)}, u32[]{:S(2)}, u32[]{:S(2)}) collective-permute-start(bf16[4,4,16,512]{3,2,1,0:T(8,128)(2,1)S(1)} %get-tuple-element.43), channel_id=1, source_target_pairs={{0,1},{1,0},{2,3},{3,2},{4,5},{5,4},{6,7},{7,6},{8,9},{9,8},{10,11... | collective-permute-start | bytes 786440 | tf_op jit(solution)/shard_map/ppermute | solution.py:243
  20.6 0.5 %collective-permute-start.4 = (bf16[4,4,16,512]{3,2,1,0:T(8,128)(2,1)S(1)}, bf16[4,4,16,512]{3,2,1,0:T(8,128)(2,1)S(1)}, u32[]{:S(2)}, u32[]{:S(2)}) collective-permute-start(bf16[4,4,16,512]{3,2,1,0:T(8,128)(2,1)S(1)} %get-tuple-element.42), channel_id=1, source_target_pairs={{0,3},{1,2},{2,1},{3,0},{4,7},{5,6},{6,5},{7,4},{8,11},{9,10},{10,... | collective-permute-start | bytes 786440 | tf_op jit(solution)/shard_map/ppermute | solution.py:243
  21.1 2.0 %rules_first.1 = (f32[2,1024,128]{2,1,0:T(8,128)S(1)}, f32[2,200,1024]{2,1,0:T(8,128)S(1)}) custom-call(bf16[4,4,16,512]{3,2,1,0:T(8,128)(2,1)S(1)} %get-tuple-element.28.refs_0_, bf16[4,4,16,512]{3,2,1,0:T(8,128)(2,1)S(1)} %collective-permute-done.refs_1_, ...), custom_call_target="tpu_custom_call", output_to_operand_aliasing={{0}: (8, {}), {1}: (9, {})} | custom-call | tf_op jit(solution)/shard_map/rules_first/pallas_call | solution.py:205
  23.1 0.9 %collective-permute-done.3.refs_0_ = bf16[4,4,16,512]{3,2,1,0:T(8,128)(2,1)S(1)} collective-permute-done((bf16[4,4,16,512]{3,2,1,0:T(8,128)(2,1)S(1)}, bf16[4,4,16,512]{3,2,1,0:T(8,128)(2,1)S(1)}, u32[]{:S(2)}, u32[]{:S(2)}) %collective-permute-start.3) | collective-permute-done | bytes 262176 | tf_op jit(solution)/shard_map/ppermute | solution.py:243
  24.0 2.1 %rules_gather.1 = (f32[2,1024,128]{2,1,0:T(8,128)S(1)}, f32[2,200,1024]{2,1,0:T(8,128)S(1)}) custom-call(bf16[4,4,16,512]{3,2,1,0:T(8,128)(2,1)S(1)} %collective-permute-done.3.refs_0_, bf16[512,2048]{1,0:T(8,128)(2,1)S(1)} %get-tuple-element.32.refs_4_.refs_1_.refs_2_, ...), custom_call_target="tpu_custom_call", output_to_operand_aliasing={{0}: (5, {}), {1}: (6, {})} | custom-call | tf_op jit(solution)/shard_map/rules_gather/pallas_call | solution.py:205
  26.1 1.1 %rules_middle.1 = (f32[2,1024,128]{2,1,0:T(8,128)S(1)}, bf16[512,2048]{1,0:T(8,128)(2,1)S(1)}, bf16[512,200]{1,0:T(8,128)(2,1)S(1)}) custom-call(bf16[4,4,16,512]{3,2,1,0:T(8,128)(2,1)S(1)} %collective-permute-done.5.refs_0_, bf16[512,2048]{1,0:T(8,128)(2,1)S(1)} %get-tuple-element.32.refs_4_.refs_1_.refs_2_, ...), custom_call_target="tpu_custom_call", output_to_operand_aliasing={{0}: (5, {})} | custom-call | tf_op jit(solution)/shard_map/rules_middle/pallas_call | solution.py:205
  27.3 1.0 %collective-permute-done.4.refs_1_ = bf16[4,4,16,512]{3,2,1,0:T(8,128)(2,1)S(1)} collective-permute-done((bf16[4,4,16,512]{3,2,1,0:T(8,128)(2,1)S(1)}, bf16[4,4,16,512]{3,2,1,0:T(8,128)(2,1)S(1)}, u32[]{:S(2)}, u32[]{:S(2)}) %collective-permute-start.4) | collective-permute-done | bytes 262176 | tf_op jit(solution)/shard_map/ppermute | solution.py:243
  28.3 1.9 %rules_last.1 = (bf16[1,200,1024]{2,1,0:T(8,128)(2,1)S(1)}, f32[2,1024,128]{2,1,0:T(8,128)S(1)}, bf16[512,2048]{1,0:T(8,128)(2,1)S(1)}, bf16[512,200]{1,0:T(8,128)(2,1)S(1)}) custom-call(f32[2,200,1024]{2,1,0:T(8,128)S(1)} %get-tuple-element.41.refs_0_.acc_ref, ...), custom_call_target="tpu_custom_call", output_to_operand_aliasing={{1}: (6, {}), {2}: (7, {}), {3}: (8, {})} | custom-call | tf_op jit(solution)/shard_map/rules_last/pallas_call | solution.py:205
  30.2 1.2 %collective-permute-start.6 = (bf16[200,1024]{1,0:T(8,128)(2,1)S(1)}, bf16[200,1024]{1,0:T(8,128)(2,1)S(1)}, u32[]{:S(2)}, u32[]{:S(2)}) collective-permute-start(bf16[200,1024]{1,0:T(8,128)(2,1)S(1)} %bitcast.13), channel_id=1, source_target_pairs={{0,16},{16,0},{1,17},{17,1},{2,18},{18,2},{3,19},{19,3},{4,20},{20... | collective-permute-start | bytes 1228808 | tf_op jit(solution)/shard_map/ppermute | solution.py:308
  31.4 1.6 %rules_finish.1 = (bf16[16,64,200]{2,1,0:T(8,128)(2,1)}, f32[200,1024]{1,0:T(8,128)S(1)}) custom-call(bf16[512,2048]{1,0:T(8,128)(2,1)S(1)} %get-tuple-element.48.feat, bf16[512,200]{1,0:T(8,128)(2,1)S(1)} %get-tuple-element.49.slope, f32[2,200,1024]{2,1,0:T(8,128)S(1)} %get-tuple-element.41.refs_0_.acc_ref, f32[2,1024,128]{2,1,0:T(8,128)S(1)} %get-tuple-element.50.disp_ref), custom_call_target="tpu_custom_call" | custom-call | tf_op jit(solution)/shard_map/rules_finish/pallas_call | solution.py:205
  32.9 1.0 %add_bitcast_fusion = f32[1,1024,200]{1,2,0:T(8,128)} fusion(f32[200,1024]{1,0:T(8,128)S(1)} %get-tuple-element.52, bf16[200,1024]{1,0:T(8,128)(2,1)S(1)} %collective-permute-done.6), kind=kLoop, calls=%fused_computation | loop fusion | flops 409600 | bytes 2048000 | tf_op jit(solution)/shard_map/broadcast_in_dim | solution.py:309
  (9 shorter events, 0.1 us)
Async XLA Ops:
  0.6 1.2 %copy-start.1 = (bf16[4,256,512]{2,1,0:T(8,128)(2,1)S(1)}, bf16[4,256,512]{2,1,0:T(8,128)(2,1)}, u32[]{:S(2)}) copy-start(bf16[4,256,512]{2,1,0:T(8,128)(2,1)} %param.5) | copy-start | bytes 3145732
  1.9 11.4 %collective-permute-start = (bf16[4,4,16,512]{3,2,1,0:T(8,128)(2,1)S(1)}, bf16[4,4,16,512]{3,2,1,0:T(8,128)(2,1)S(1)}, u32[]{:S(2)}, u32[]{:S(2)}) collective-permute-start(bf16[4,4,16,512]{3,2,1,0:T(8,128)(2,1)S(1)} %get-tuple-element.29), channel_id=1, source_target_pairs={{0,8},{1,9},{2,10},{3,11},{4,12},{5,13},{6,14},{7,15},{8,0},{9,1},... | collective-permute-start | bytes 786440 | tf_op jit(solution)/shard_map/ppermute | solution.py:243
  6.0 7.7 %collective-permute-start.1 = (bf16[4,4,16,512]{3,2,1,0:T(8,128)(2,1)S(1)}, bf16[4,4,16,512]{3,2,1,0:T(8,128)(2,1)S(1)}, u32[]{:S(2)}, u32[]{:S(2)}) collective-permute-start(bf16[4,4,16,512]{3,2,1,0:T(8,128)(2,1)S(1)} %get-tuple-element.30), channel_id=1, source_target_pairs={{0,4},{1,5},{2,6},{3,7},{4,0},{5,1},{6,2},{7,3},{8,12},{9,13},{10,... | collective-permute-start | bytes 786440 | tf_op jit(solution)/shard_map/ppermute | solution.py:243
  7.6 9.9 %collective-permute-start.2 = (bf16[4,4,16,512]{3,2,1,0:T(8,128)(2,1)S(1)}, bf16[4,4,16,512]{3,2,1,0:T(8,128)(2,1)S(1)}, u32[]{:S(2)}, u32[]{:S(2)}) collective-permute-start(bf16[4,4,16,512]{3,2,1,0:T(8,128)(2,1)S(1)} %get-tuple-element.31), channel_id=1, source_target_pairs={{0,12},{1,13},{2,14},{3,15},{4,8},{5,9},{6,10},{7,11},{8,4},{9,5},... | collective-permute-start | bytes 786440 | tf_op jit(solution)/shard_map/ppermute | solution.py:243
  7.6 1.6 %copy-start = (bf16[512,2048]{1,0:T(8,128)(2,1)S(1)}, bf16[512,2048]{1,0:T(8,128)(2,1)}, u32[]{:S(2)}) copy-start(bf16[512,2048]{1,0:T(8,128)(2,1)} %refs_0_.1) | copy-start | bytes 6291460
  9.2 1.1 %copy-start.2 = (bf16[1,2048,200]{1,2,0:T(8,128)(2,1)S(1)}, bf16[1,2048,200]{1,2,0:T(8,128)(2,1)}, u32[]{:S(2)}) copy-start(bf16[1,2048,200]{1,2,0:T(8,128)(2,1)} %param.8) | copy-start | bytes 2457604
  10.3 0.9 %copy-start.3 = (bf16[512,200]{0,1:T(8,128)(2,1)S(1)}, bf16[512,200]{0,1:T(8,128)(2,1)}, u32[]{:S(2)}) copy-start(bf16[512,200]{0,1:T(8,128)(2,1)} %param.7) | copy-start | bytes 614404
  11.3 0.7 %copy-start.4 = (f32[1,200]{1,0:T(1,128)S(1)}, f32[1,200]{1,0:T(1,128)}, u32[]{:S(2)}) copy-start(f32[1,200]{1,0:T(1,128)} %refs_3_.1) | copy-start | bytes 2404
  17.6 6.4 %collective-permute-start.3 = (bf16[4,4,16,512]{3,2,1,0:T(8,128)(2,1)S(1)}, bf16[4,4,16,512]{3,2,1,0:T(8,128)(2,1)S(1)}, u32[]{:S(2)}, u32[]{:S(2)}) collective-permute-start(bf16[4,4,16,512]{3,2,1,0:T(8,128)(2,1)S(1)} %get-tuple-element.36), channel_id=1, source_target_pairs={{0,2},{1,3},{2,0},{3,1},{4,6},{5,7},{6,4},{7,5},{8,10},{9,11},{10,... | collective-permute-start | bytes 786440 | tf_op jit(solution)/shard_map/ppermute | solution.py:243
  19.1 7.0 %collective-permute-start.5 = (bf16[4,4,16,512]{3,2,1,0:T(8,128)(2,1)S(1)}, bf16[4,4,16,512]{3,2,1,0:T(8,128)(2,1)S(1)}, u32[]{:S(2)}, u32[]{:S(2)}) collective-permute-start(bf16[4,4,16,512]{3,2,1,0:T(8,128)(2,1)S(1)} %get-tuple-element.43), channel_id=1, source_target_pairs={{0,1},{1,0},{2,3},{3,2},{4,5},{5,4},{6,7},{7,6},{8,9},{9,8},{10,11... | collective-permute-start | bytes 786440 | tf_op jit(solution)/shard_map/ppermute | solution.py:243
  20.6 7.6 %collective-permute-start.4 = (bf16[4,4,16,512]{3,2,1,0:T(8,128)(2,1)S(1)}, bf16[4,4,16,512]{3,2,1,0:T(8,128)(2,1)S(1)}, u32[]{:S(2)}, u32[]{:S(2)}) collective-permute-start(bf16[4,4,16,512]{3,2,1,0:T(8,128)(2,1)S(1)} %get-tuple-element.42), channel_id=1, source_target_pairs={{0,3},{1,2},{2,1},{3,0},{4,7},{5,6},{6,5},{7,4},{8,11},{9,10},{10,... | collective-permute-start | bytes 786440 | tf_op jit(solution)/shard_map/ppermute | solution.py:243
  30.2 2.7 %collective-permute-start.6 = (bf16[200,1024]{1,0:T(8,128)(2,1)S(1)}, bf16[200,1024]{1,0:T(8,128)(2,1)S(1)}, u32[]{:S(2)}, u32[]{:S(2)}) collective-permute-start(bf16[200,1024]{1,0:T(8,128)(2,1)S(1)} %bitcast.13), channel_id=1, source_target_pairs={{0,16},{16,0},{1,17},{17,1},{2,18},{18,2},{3,19},{19,3},{4,20},{20... | collective-permute-start | bytes 1228808 | tf_op jit(solution)/shard_map/ppermute | solution.py:308

commit v5 on v4

--- a/solution.py
+++ b/solution.py
@@ -26,14 +26,6 @@
 
 def cuts_of(regions):
     return [(i, c, min(LANES, regions - c)) for i, c in enumerate(range(0, regions, LANES))]
-
-
-def run_copies(moves, sem):
-    copies = [pltpu.make_async_copy(a, b, sem.at[i]) for i, (a, b) in enumerate(moves)]
-    for c in copies:
-        c.start()
-    for c in copies:
-        c.wait()
 
 
 def flips(groups, blocks):
@@ -125,8 +117,9 @@
 
 
 def load_kernel(*refs):
-    k = (len(refs) - 1) // 2
-    run_copies(list(zip(refs[:k], refs[k:-1])), refs[-1])
+    k = len(refs) // 2
+    for source, out in zip(refs[:k], refs[k:]):
+        out[...] = source[...]
 
 
 def own_digit(cfg, parts, weights, disp_ref, acc_ref, slope, feat):
@@ -199,13 +192,12 @@
             dec_ref[h, :, pl.ds(c, w)] = disp_ref[i, pl.ds(h, paths, stride=hour_blk), :][:, :w].astype(BF16)
 
 
-def call(kernel, name, outs, operands, scratch=(), aliases=None, in_hbm=0):
+def call(kernel, name, outs, operands, scratch=(), aliases=None):
     vmem = pl.BlockSpec(memory_space=pltpu.VMEM)
-    hbm = pl.BlockSpec(memory_space=pl.ANY)
     return pl.pallas_call(
         kernel,
         out_shape=tuple(outs),
-        in_specs=[hbm] * in_hbm + [vmem] * (len(operands) - in_hbm),
+        in_specs=[vmem] * len(operands),
         out_specs=[vmem] * len(outs),
         scratch_shapes=list(scratch),
         input_output_aliases=aliases or {},
@@ -252,7 +244,6 @@
     weights = (loadings, netload_map.T, rule_weights[0].T, rule_bias)
     weights = call(
         load_kernel, "load", [jax.ShapeDtypeStruct(w.shape, w.dtype) for w in weights], weights,
-        [pltpu.SemaphoreType.DMA((len(weights),))], in_hbm=len(weights),
     )
     disp_shape = f32(pl.cdiv(regions, LANES), rows, LANES)
     acc_shape = f32(groups, regions, share)

time: 34.5 us -> 34.5 us (level)
  transfers between devices with their start and end apart: 7 -> 7, of which waited for: 5 -> 5; matrix products, arithmetic and copies ran while one was open for 0% -> 0% of each run, Pallas kernels for 22% -> 21%
where the time goes in v5:
time: 34.5 us; the launch traced here: 33.9 us
  starting transfers between devices  10.4 us (30%)
  Pallas kernels  9.01 us (26%)
  waiting for transfers between devices  7.24 us (21%)
  local copies, waits for them, and re-layouts  5.56 us (16%)
  other arithmetic  1.02 us (3%)
  between operations  0.7 us (2%)
    ppermute x6, starting transfers between devices, hop(): return lax.ppermute(x, ('grp', 'blk'), pairs)  9.23 us
    pallas_call x8, Pallas kernels, call(): pl.pallas_call(kernel, out_shape=tuple(outs), in_specs=[vmem] * len(opera...  9.01 us
    ppermute x6, waiting for transfers between devices, hop(): return lax.ppermute(x, ('grp', 'blk'), pairs)  7.24 us
    unnamed x10, local copies, waits for them, and re-layouts  5.56 us
    ppermute x1, starting transfers between devices, body(): grad = grad + lax.ppermute(send[step - 1], 'grp', pairs).astype(F32)  1.17 us
    broadcast_in_dim x1, other arithmetic, body(): return (decisions, grad.T[None])  1.02 us
  transfers between devices with their start and end apart: 7, of which 5 were waited for; matrix products, arithmetic and copies ran while one was open for 0% of the time, Pallas kernels for 21%

profile of v5, /device:TPU:0, one launch (start us, length us, event | category | flops | bytes accessed | tf_op | source)
XLA Modules:
  0.0 33.9 jit_solution(9169095753274328540)
XLA Ops:
  0.6 1.2 %copy-done.1 = bf16[4,256,512]{2,1,0:T(8,128)(2,1)S(1)} copy-done((bf16[4,256,512]{2,1,0:T(8,128)(2,1)S(1)}, bf16[4,256,512]{2,1,0:T(8,128)(2,1)}, u32[]{:S(2)}) %copy-start.1) | copy-done | bytes 1048600
  1.9 0.1 pack.1
  1.9 4.1 %collective-permute-start = (bf16[4,4,16,512]{3,2,1,0:T(8,128)(2,1)S(1)}, bf16[4,4,16,512]{3,2,1,0:T(8,128)(2,1)S(1)}, u32[]{:S(2)}, u32[]{:S(2)}) collective-permute-start(bf16[4,4,16,512]{3,2,1,0:T(8,128)(2,1)S(1)} %get-tuple-element.29), channel_id=1, source_target_pairs={{0,8},{1,9},{2,10},{3,11},{4,12},{5,13},{6,14},{7,15},{8,0},{9,1},... | collective-permute-start | bytes 786440 | tf_op jit(solution)/shard_map/ppermute | solution.py:235
  6.0 1.6 %collective-permute-start.1 = (bf16[4,4,16,512]{3,2,1,0:T(8,128)(2,1)S(1)}, bf16[4,4,16,512]{3,2,1,0:T(8,128)(2,1)S(1)}, u32[]{:S(2)}, u32[]{:S(2)}) collective-permute-start(bf16[4,4,16,512]{3,2,1,0:T(8,128)(2,1)S(1)} %get-tuple-element.30), channel_id=1, source_target_pairs={{0,4},{1,5},{2,6},{3,7},{4,0},{5,1},{6,2},{7,3},{8,12},{9,13},{10,... | collective-permute-start | bytes 786440 | tf_op jit(solution)/shard_map/ppermute | solution.py:235
  7.6 1.6 %copy-done = bf16[512,2048]{1,0:T(8,128)(2,1)S(1)} copy-done((bf16[512,2048]{1,0:T(8,128)(2,1)S(1)}, bf16[512,2048]{1,0:T(8,128)(2,1)}, u32[]{:S(2)}) %copy-start) | copy-done | bytes 2097176
  9.2 1.1 %copy-done.2 = bf16[1,2048,200]{1,2,0:T(8,128)(2,1)S(1)} copy-done((bf16[1,2048,200]{1,2,0:T(8,128)(2,1)S(1)}, bf16[1,2048,200]{1,2,0:T(8,128)(2,1)}, u32[]{:S(2)}) %copy-start.2) | copy-done | bytes 819224
  10.3 0.9 %copy-done.3 = bf16[512,200]{0,1:T(8,128)(2,1)S(1)} copy-done((bf16[512,200]{0,1:T(8,128)(2,1)S(1)}, bf16[512,200]{0,1:T(8,128)(2,1)}, u32[]{:S(2)}) %copy-start.3) | copy-done | bytes 204824
  11.3 0.7 %copy-done.4 = f32[1,200]{1,0:T(1,128)S(1)} copy-done((f32[1,200]{1,0:T(1,128)S(1)}, f32[1,200]{1,0:T(1,128)}, u32[]{:S(2)}) %copy-start.4) | copy-done | bytes 824
  12.0 0.2 load.1
  12.2 1.1 %collective-permute-done.refs_1_ = bf16[4,4,16,512]{3,2,1,0:T(8,128)(2,1)S(1)} collective-permute-done((bf16[4,4,16,512]{3,2,1,0:T(8,128)(2,1)S(1)}, bf16[4,4,16,512]{3,2,1,0:T(8,128)(2,1)S(1)}, u32[]{:S(2)}, u32[]{:S(2)}) %collective-permute-start) | collective-permute-done | bytes 262176 | tf_op jit(solution)/shard_map/ppermute | solution.py:235
  13.3 0.5 %collective-permute-done.1.refs_2_ = bf16[4,4,16,512]{3,2,1,0:T(8,128)(2,1)S(1)} collective-permute-done((bf16[4,4,16,512]{3,2,1,0:T(8,128)(2,1)S(1)}, bf16[4,4,16,512]{3,2,1,0:T(8,128)(2,1)S(1)}, u32[]{:S(2)}, u32[]{:S(2)}) %collective-permute-start.1) | collective-permute-done | bytes 262176 | tf_op jit(solution)/shard_map/ppermute | solution.py:235
  13.8 3.7 %collective-permute-done.2.refs_3_ = bf16[4,4,16,512]{3,2,1,0:T(8,128)(2,1)S(1)} collective-permute-done((bf16[4,4,16,512]{3,2,1,0:T(8,128)(2,1)S(1)}, bf16[4,4,16,512]{3,2,1,0:T(8,128)(2,1)S(1)}, u32[]{:S(2)}, u32[]{:S(2)}) %collective-permute-start.2) | collective-permute-done | bytes 262176 | tf_op jit(solution)/shard_map/ppermute | solution.py:235
  17.6 1.6 %collective-permute-start.3 = (bf16[4,4,16,512]{3,2,1,0:T(8,128)(2,1)S(1)}, bf16[4,4,16,512]{3,2,1,0:T(8,128)(2,1)S(1)}, u32[]{:S(2)}, u32[]{:S(2)}) collective-permute-start(bf16[4,4,16,512]{3,2,1,0:T(8,128)(2,1)S(1)} %get-tuple-element.36), channel_id=1, source_target_pairs={{0,2},{1,3},{2,0},{3,1},{4,6},{5,7},{6,4},{7,5},{8,10},{9,11},{10,... | collective-permute-start | bytes 786440 | tf_op jit(solution)/shard_map/ppermute | solution.py:235
  19.1 1.5 %collective-permute-start.5 = (bf16[4,4,16,512]{3,2,1,0:T(8,128)(2,1)S(1)}, bf16[4,4,16,512]{3,2,1,0:T(8,128)(2,1)S(1)}, u32[]{:S(2)}, u32[]{:S(2)}) collective-permute-start(bf16[4,4,16,512]{3,2,1,0:T(8,128)(2,1)S(1)} %get-tuple-element.43), channel_id=1, source_target_pairs={{0,1},{1,0},{2,3},{3,2},{4,5},{5,4},{6,7},{7,6},{8,9},{9,8},{10,11... | collective-permute-start | bytes 786440 | tf_op jit(solution)/shard_map/ppermute | solution.py:235
  20.6 0.5 %collective-permute-start.4 = (bf16[4,4,16,512]{3,2,1,0:T(8,128)(2,1)S(1)}, bf16[4,4,16,512]{3,2,1,0:T(8,128)(2,1)S(1)}, u32[]{:S(2)}, u32[]{:S(2)}) collective-permute-start(bf16[4,4,16,512]{3,2,1,0:T(8,128)(2,1)S(1)} %get-tuple-element.42), channel_id=1, source_target_pairs={{0,3},{1,2},{2,1},{3,0},{4,7},{5,6},{6,5},{7,4},{8,11},{9,10},{10,... | collective-permute-start | bytes 786440 | tf_op jit(solution)/shard_map/ppermute | solution.py:235
  21.1 2.0 %rules_first.1 = (f32[2,1024,128]{2,1,0:T(8,128)S(1)}, f32[2,200,1024]{2,1,0:T(8,128)S(1)}) custom-call(bf16[4,4,16,512]{3,2,1,0:T(8,128)(2,1)S(1)} %get-tuple-element.28.refs_0_, bf16[4,4,16,512]{3,2,1,0:T(8,128)(2,1)S(1)} %collective-permute-done.refs_1_, ...), custom_call_target="tpu_custom_call", output_to_operand_aliasing={{0}: (8, {}), {1}: (9, {})} | custom-call | tf_op jit(solution)/shard_map/rules_first/pallas_call | solution.py:197
  23.1 0.9 %collective-permute-done.3.refs_0_ = bf16[4,4,16,512]{3,2,1,0:T(8,128)(2,1)S(1)} collective-permute-done((bf16[4,4,16,512]{3,2,1,0:T(8,128)(2,1)S(1)}, bf16[4,4,16,512]{3,2,1,0:T(8,128)(2,1)S(1)}, u32[]{:S(2)}, u32[]{:S(2)}) %collective-permute-start.3) | collective-permute-done | bytes 262176 | tf_op jit(solution)/shard_map/ppermute | solution.py:235
  24.0 2.1 %rules_gather.1 = (f32[2,1024,128]{2,1,0:T(8,128)S(1)}, f32[2,200,1024]{2,1,0:T(8,128)S(1)}) custom-call(bf16[4,4,16,512]{3,2,1,0:T(8,128)(2,1)S(1)} %collective-permute-done.3.refs_0_, bf16[512,2048]{1,0:T(8,128)(2,1)S(1)} %get-tuple-element.32.refs_4_.refs_1_.refs_2_, ...), custom_call_target="tpu_custom_call", output_to_operand_aliasing={{0}: (5, {}), {1}: (6, {})} | custom-call | tf_op jit(solution)/shard_map/rules_gather/pallas_call | solution.py:197
  26.1 1.1 %rules_middle.1 = (f32[2,1024,128]{2,1,0:T(8,128)S(1)}, bf16[512,2048]{1,0:T(8,128)(2,1)S(1)}, bf16[512,200]{1,0:T(8,128)(2,1)S(1)}) custom-call(bf16[4,4,16,512]{3,2,1,0:T(8,128)(2,1)S(1)} %collective-permute-done.5.refs_0_, bf16[512,2048]{1,0:T(8,128)(2,1)S(1)} %get-tuple-element.32.refs_4_.refs_1_.refs_2_, ...), custom_call_target="tpu_custom_call", output_to_operand_aliasing={{0}: (5, {})} | custom-call | tf_op jit(solution)/shard_map/rules_middle/pallas_call | solution.py:197
  27.3 1.0 %collective-permute-done.4.refs_1_ = bf16[4,4,16,512]{3,2,1,0:T(8,128)(2,1)S(1)} collective-permute-done((bf16[4,4,16,512]{3,2,1,0:T(8,128)(2,1)S(1)}, bf16[4,4,16,512]{3,2,1,0:T(8,128)(2,1)S(1)}, u32[]{:S(2)}, u32[]{:S(2)}) %collective-permute-start.4) | collective-permute-done | bytes 262176 | tf_op jit(solution)/shard_map/ppermute | solution.py:235
  28.3 1.9 %rules_last.1 = (bf16[1,200,1024]{2,1,0:T(8,128)(2,1)S(1)}, f32[2,1024,128]{2,1,0:T(8,128)S(1)}, bf16[512,2048]{1,0:T(8,128)(2,1)S(1)}, bf16[512,200]{1,0:T(8,128)(2,1)S(1)}) custom-call(f32[2,200,1024]{2,1,0:T(8,128)S(1)} %get-tuple-element.41.refs_0_.acc_ref, ...), custom_call_target="tpu_custom_call", output_to_operand_aliasing={{1}: (6, {}), {2}: (7, {}), {3}: (8, {})} | custom-call | tf_op jit(solution)/shard_map/rules_last/pallas_call | solution.py:197
  30.2 1.2 %collective-permute-start.6 = (bf16[200,1024]{1,0:T(8,128)(2,1)S(1)}, bf16[200,1024]{1,0:T(8,128)(2,1)S(1)}, u32[]{:S(2)}, u32[]{:S(2)}) collective-permute-start(bf16[200,1024]{1,0:T(8,128)(2,1)S(1)} %bitcast.13), channel_id=1, source_target_pairs={{0,16},{16,0},{1,17},{17,1},{2,18},{18,2},{3,19},{19,3},{4,20},{20... | collective-permute-start | bytes 1228808 | tf_op jit(solution)/shard_map/ppermute | solution.py:299
  31.4 1.6 %rules_finish.1 = (bf16[16,64,200]{2,1,0:T(8,128)(2,1)}, f32[200,1024]{1,0:T(8,128)S(1)}) custom-call(bf16[512,2048]{1,0:T(8,128)(2,1)S(1)} %get-tuple-element.48.feat, bf16[512,200]{1,0:T(8,128)(2,1)S(1)} %get-tuple-element.49.slope, f32[2,200,1024]{2,1,0:T(8,128)S(1)} %get-tuple-element.41.refs_0_.acc_ref, f32[2,1024,128]{2,1,0:T(8,128)S(1)} %get-tuple-element.50.disp_ref), custom_call_target="tpu_custom_call" | custom-call | tf_op jit(solution)/shard_map/rules_finish/pallas_call | solution.py:197
  32.9 1.0 %add_bitcast_fusion = f32[1,1024,200]{1,2,0:T(8,128)} fusion(f32[200,1024]{1,0:T(8,128)S(1)} %get-tuple-element.52, bf16[200,1024]{1,0:T(8,128)(2,1)S(1)} %collective-permute-done.6), kind=kLoop, calls=%fused_computation | loop fusion | flops 409600 | bytes 2048000 | tf_op jit(solution)/shard_map/broadcast_in_dim | solution.py:300
  (9 shorter events, 0.1 us)
Async XLA Ops:
  0.6 1.2 %copy-start.1 = (bf16[4,256,512]{2,1,0:T(8,128)(2,1)S(1)}, bf16[4,256,512]{2,1,0:T(8,128)(2,1)}, u32[]{:S(2)}) copy-start(bf16[4,256,512]{2,1,0:T(8,128)(2,1)} %param.5) | copy-start | bytes 3145732
  1.9 11.4 %collective-permute-start = (bf16[4,4,16,512]{3,2,1,0:T(8,128)(2,1)S(1)}, bf16[4,4,16,512]{3,2,1,0:T(8,128)(2,1)S(1)}, u32[]{:S(2)}, u32[]{:S(2)}) collective-permute-start(bf16[4,4,16,512]{3,2,1,0:T(8,128)(2,1)S(1)} %get-tuple-element.29), channel_id=1, source_target_pairs={{0,8},{1,9},{2,10},{3,11},{4,12},{5,13},{6,14},{7,15},{8,0},{9,1},... | collective-permute-start | bytes 786440 | tf_op jit(solution)/shard_map/ppermute | solution.py:235
  6.0 7.7 %collective-permute-start.1 = (bf16[4,4,16,512]{3,2,1,0:T(8,128)(2,1)S(1)}, bf16[4,4,16,512]{3,2,1,0:T(8,128)(2,1)S(1)}, u32[]{:S(2)}, u32[]{:S(2)}) collective-permute-start(bf16[4,4,16,512]{3,2,1,0:T(8,128)(2,1)S(1)} %get-tuple-element.30), channel_id=1, source_target_pairs={{0,4},{1,5},{2,6},{3,7},{4,0},{5,1},{6,2},{7,3},{8,12},{9,13},{10,... | collective-permute-start | bytes 786440 | tf_op jit(solution)/shard_map/ppermute | solution.py:235
  7.6 9.9 %collective-permute-start.2 = (bf16[4,4,16,512]{3,2,1,0:T(8,128)(2,1)S(1)}, bf16[4,4,16,512]{3,2,1,0:T(8,128)(2,1)S(1)}, u32[]{:S(2)}, u32[]{:S(2)}) collective-permute-start(bf16[4,4,16,512]{3,2,1,0:T(8,128)(2,1)S(1)} %get-tuple-element.31), channel_id=1, source_target_pairs={{0,12},{1,13},{2,14},{3,15},{4,8},{5,9},{6,10},{7,11},{8,4},{9,5},... | collective-permute-start | bytes 786440 | tf_op jit(solution)/shard_map/ppermute | solution.py:235
  7.6 1.6 %copy-start = (bf16[512,2048]{1,0:T(8,128)(2,1)S(1)}, bf16[512,2048]{1,0:T(8,128)(2,1)}, u32[]{:S(2)}) copy-start(bf16[512,2048]{1,0:T(8,128)(2,1)} %refs_0_.1) | copy-start | bytes 6291460
  9.2 1.1 %copy-start.2 = (bf16[1,2048,200]{1,2,0:T(8,128)(2,1)S(1)}, bf16[1,2048,200]{1,2,0:T(8,128)(2,1)}, u32[]{:S(2)}) copy-start(bf16[1,2048,200]{1,2,0:T(8,128)(2,1)} %param.8) | copy-start | bytes 2457604
  10.3 0.9 %copy-start.3 = (bf16[512,200]{0,1:T(8,128)(2,1)S(1)}, bf16[512,200]{0,1:T(8,128)(2,1)}, u32[]{:S(2)}) copy-start(bf16[512,200]{0,1:T(8,128)(2,1)} %param.7) | copy-start | bytes 614404
  11.3 0.7 %copy-start.4 = (f32[1,200]{1,0:T(1,128)S(1)}, f32[1,200]{1,0:T(1,128)}, u32[]{:S(2)}) copy-start(f32[1,200]{1,0:T(1,128)} %refs_3_.1) | copy-start | bytes 2404
  17.6 6.4 %collective-permute-start.3 = (bf16[4,4,16,512]{3,2,1,0:T(8,128)(2,1)S(1)}, bf16[4,4,16,512]{3,2,1,0:T(8,128)(2,1)S(1)}, u32[]{:S(2)}, u32[]{:S(2)}) collective-permute-start(bf16[4,4,16,512]{3,2,1,0:T(8,128)(2,1)S(1)} %get-tuple-element.36), channel_id=1, source_target_pairs={{0,2},{1,3},{2,0},{3,1},{4,6},{5,7},{6,4},{7,5},{8,10},{9,11},{10,... | collective-permute-start | bytes 786440 | tf_op jit(solution)/shard_map/ppermute | solution.py:235
  19.1 7.0 %collective-permute-start.5 = (bf16[4,4,16,512]{3,2,1,0:T(8,128)(2,1)S(1)}, bf16[4,4,16,512]{3,2,1,0:T(8,128)(2,1)S(1)}, u32[]{:S(2)}, u32[]{:S(2)}) collective-permute-start(bf16[4,4,16,512]{3,2,1,0:T(8,128)(2,1)S(1)} %get-tuple-element.43), channel_id=1, source_target_pairs={{0,1},{1,0},{2,3},{3,2},{4,5},{5,4},{6,7},{7,6},{8,9},{9,8},{10,11... | collective-permute-start | bytes 786440 | tf_op jit(solution)/shard_map/ppermute | solution.py:235
  20.6 7.6 %collective-permute-start.4 = (bf16[4,4,16,512]{3,2,1,0:T(8,128)(2,1)S(1)}, bf16[4,4,16,512]{3,2,1,0:T(8,128)(2,1)S(1)}, u32[]{:S(2)}, u32[]{:S(2)}) collective-permute-start(bf16[4,4,16,512]{3,2,1,0:T(8,128)(2,1)S(1)} %get-tuple-element.42), channel_id=1, source_target_pairs={{0,3},{1,2},{2,1},{3,0},{4,7},{5,6},{6,5},{7,4},{8,11},{9,10},{10,... | collective-permute-start | bytes 786440 | tf_op jit(solution)/shard_map/ppermute | solution.py:235
  30.2 2.7 %collective-permute-start.6 = (bf16[200,1024]{1,0:T(8,128)(2,1)S(1)}, bf16[200,1024]{1,0:T(8,128)(2,1)S(1)}, u32[]{:S(2)}, u32[]{:S(2)}) collective-permute-start(bf16[200,1024]{1,0:T(8,128)(2,1)S(1)} %bitcast.13), channel_id=1, source_target_pairs={{0,16},{16,0},{1,17},{17,1},{2,18},{18,2},{3,19},{19,3},{4,20},{20... | collective-permute-start | bytes 1228808 | tf_op jit(solution)/shard_map/ppermute | solution.py:299

commit v6 on v5

--- a/solution.py
+++ b/solution.py
@@ -192,6 +192,23 @@
             dec_ref[h, :, pl.ds(c, w)] = disp_ref[i, pl.ds(h, paths, stride=hour_blk), :][:, :w].astype(BF16)
 
 
+def add_kernel(own_ref, *refs):
+    received, out, stage, sem = refs[:-3], refs[-3], refs[-2], refs[-1]
+    n = sem.shape[0]
+    width = own_ref.shape[1] // n
+    copies = []
+    for i in range(n):
+        cols = pl.ds(i * width, width)
+        total = own_ref[:, cols]
+        for r in received:
+            total = total + r[:, cols].astype(F32)
+        stage[:, cols] = total
+        copies.append(pltpu.make_async_copy(stage.at[:, cols], out.at[:, cols], sem.at[i]))
+        copies[-1].start()
+    for c in copies:
+        c.wait()
+
+
 def call(kernel, name, outs, operands, scratch=(), aliases=None):
     vmem = pl.BlockSpec(memory_space=pltpu.VMEM)
     return pl.pallas_call(
@@ -294,9 +311,17 @@
         functools.partial(finish_kernel, groups, row_scale), "rules_finish",
         [bf(hour_blk, paths, regions), f32(regions, share)], [feat, slope, acc, disp],
     )
+    received = []
     for step in range(1, groups):
         pairs = [(g, (g + step) % groups) for g in range(groups)]
-        grad = grad + lax.ppermute(send[step - 1], "grp", pairs).astype(F32)
+        received.append(lax.ppermute(send[step - 1], "grp", pairs))
+    vmem, hbm = pl.BlockSpec(memory_space=pltpu.VMEM), pl.BlockSpec(memory_space=pl.ANY)
+    chunks = block_of(share // LANES, 4)
+    grad = pl.pallas_call(
+        add_kernel, out_shape=f32(regions, share), in_specs=[vmem] * groups, out_specs=hbm,
+        scratch_shapes=[pltpu.VMEM((regions, share), F32), pltpu.SemaphoreType.DMA((chunks,))],
+        compiler_params=pltpu.CompilerParams(vmem_limit_bytes=16 << 20), name="add",
+    )(grad, *received)
     return decisions, grad.T[None]
 
 

time: 34.5 us -> 34.4 us (level)
  other arithmetic: 1.02 us -> 0 us
  Pallas kernels: 9.01 us -> 9.97 us
    broadcast_in_dim x1 -> x0, other arithmetic: 1.02 us -> none  [body(): return (decisions, grad.T[None])]
    pallas_call x0 -> x1, Pallas kernels: none -> 0.95 us  [body(): pl.pallas_call(add_kernel, out_shape=f32(regions, share), in_specs=[vmem]...]
where the time goes in v6:
time: 34.4 us; the launch traced here: 33.9 us
  starting transfers between devices  10.4 us (30%)
  Pallas kernels  9.97 us (29%)
  waiting for transfers between devices  7.24 us (21%)
  local copies, waits for them, and re-layouts  5.56 us (16%)
  between operations  0.7 us (2%)
    ppermute x6, starting transfers between devices, hop(): return lax.ppermute(x, ('grp', 'blk'), pairs)  9.23 us
    pallas_call x8, Pallas kernels, call(): pl.pallas_call(kernel, out_shape=tuple(outs), in_specs=[vmem] * len(opera...  9.01 us
    ppermute x6, waiting for transfers between devices, hop(): return lax.ppermute(x, ('grp', 'blk'), pairs)  7.24 us
    unnamed x10, local copies, waits for them, and re-layouts  5.56 us
    ppermute x1, starting transfers between devices, body(): received.append(lax.ppermute(send[step - 1], 'grp', pairs))  1.17 us
    pallas_call x1, Pallas kernels, body(): pl.pallas_call(add_kernel, out_shape=f32(regions, share), in_specs=[vmem]...  0.95 us
  transfers between devices with their start and end apart: 7, of which 5 were waited for; matrix products, arithmetic and copies ran while one was open for 0% of the time, Pallas kernels for 21%

profile of v6, /device:TPU:0, one launch (start us, length us, event | category | flops | bytes accessed | tf_op | source)
XLA Modules:
  0.0 33.9 jit_solution(10377694374599770958)
XLA Ops:
  0.6 1.2 %copy-done.1 = bf16[4,256,512]{2,1,0:T(8,128)(2,1)S(1)} copy-done((bf16[4,256,512]{2,1,0:T(8,128)(2,1)S(1)}, bf16[4,256,512]{2,1,0:T(8,128)(2,1)}, u32[]{:S(2)}) %copy-start.1) | copy-done | bytes 1048600
  1.9 0.1 pack.1
  1.9 4.1 %collective-permute-start = (bf16[4,4,16,512]{3,2,1,0:T(8,128)(2,1)S(1)}, bf16[4,4,16,512]{3,2,1,0:T(8,128)(2,1)S(1)}, u32[]{:S(2)}, u32[]{:S(2)}) collective-permute-start(bf16[4,4,16,512]{3,2,1,0:T(8,128)(2,1)S(1)} %get-tuple-element.29), channel_id=1, source_target_pairs={{0,8},{1,9},{2,10},{3,11},{4,12},{5,13},{6,14},{7,15},{8,0},{9,1},... | collective-permute-start | bytes 786440 | tf_op jit(solution)/shard_map/ppermute | solution.py:252
  6.0 1.6 %collective-permute-start.1 = (bf16[4,4,16,512]{3,2,1,0:T(8,128)(2,1)S(1)}, bf16[4,4,16,512]{3,2,1,0:T(8,128)(2,1)S(1)}, u32[]{:S(2)}, u32[]{:S(2)}) collective-permute-start(bf16[4,4,16,512]{3,2,1,0:T(8,128)(2,1)S(1)} %get-tuple-element.30), channel_id=1, source_target_pairs={{0,4},{1,5},{2,6},{3,7},{4,0},{5,1},{6,2},{7,3},{8,12},{9,13},{10,... | collective-permute-start | bytes 786440 | tf_op jit(solution)/shard_map/ppermute | solution.py:252
  7.6 1.6 %copy-done = bf16[512,2048]{1,0:T(8,128)(2,1)S(1)} copy-done((bf16[512,2048]{1,0:T(8,128)(2,1)S(1)}, bf16[512,2048]{1,0:T(8,128)(2,1)}, u32[]{:S(2)}) %copy-start) | copy-done | bytes 2097176
  9.2 1.1 %copy-done.2 = bf16[1,2048,200]{1,2,0:T(8,128)(2,1)S(1)} copy-done((bf16[1,2048,200]{1,2,0:T(8,128)(2,1)S(1)}, bf16[1,2048,200]{1,2,0:T(8,128)(2,1)}, u32[]{:S(2)}) %copy-start.2) | copy-done | bytes 819224
  10.3 0.9 %copy-done.3 = bf16[512,200]{0,1:T(8,128)(2,1)S(1)} copy-done((bf16[512,200]{0,1:T(8,128)(2,1)S(1)}, bf16[512,200]{0,1:T(8,128)(2,1)}, u32[]{:S(2)}) %copy-start.3) | copy-done | bytes 204824
  11.3 0.7 %copy-done.4 = f32[1,200]{1,0:T(1,128)S(1)} copy-done((f32[1,200]{1,0:T(1,128)S(1)}, f32[1,200]{1,0:T(1,128)}, u32[]{:S(2)}) %copy-start.4) | copy-done | bytes 824
  12.0 0.2 load.1
  12.2 1.1 %collective-permute-done.refs_1_ = bf16[4,4,16,512]{3,2,1,0:T(8,128)(2,1)S(1)} collective-permute-done((bf16[4,4,16,512]{3,2,1,0:T(8,128)(2,1)S(1)}, bf16[4,4,16,512]{3,2,1,0:T(8,128)(2,1)S(1)}, u32[]{:S(2)}, u32[]{:S(2)}) %collective-permute-start) | collective-permute-done | bytes 262176 | tf_op jit(solution)/shard_map/ppermute | solution.py:252
  13.3 0.5 %collective-permute-done.1.refs_2_ = bf16[4,4,16,512]{3,2,1,0:T(8,128)(2,1)S(1)} collective-permute-done((bf16[4,4,16,512]{3,2,1,0:T(8,128)(2,1)S(1)}, bf16[4,4,16,512]{3,2,1,0:T(8,128)(2,1)S(1)}, u32[]{:S(2)}, u32[]{:S(2)}) %collective-permute-start.1) | collective-permute-done | bytes 262176 | tf_op jit(solution)/shard_map/ppermute | solution.py:252
  13.8 3.7 %collective-permute-done.2.refs_3_ = bf16[4,4,16,512]{3,2,1,0:T(8,128)(2,1)S(1)} collective-permute-done((bf16[4,4,16,512]{3,2,1,0:T(8,128)(2,1)S(1)}, bf16[4,4,16,512]{3,2,1,0:T(8,128)(2,1)S(1)}, u32[]{:S(2)}, u32[]{:S(2)}) %collective-permute-start.2) | collective-permute-done | bytes 262176 | tf_op jit(solution)/shard_map/ppermute | solution.py:252
  17.6 1.6 %collective-permute-start.3 = (bf16[4,4,16,512]{3,2,1,0:T(8,128)(2,1)S(1)}, bf16[4,4,16,512]{3,2,1,0:T(8,128)(2,1)S(1)}, u32[]{:S(2)}, u32[]{:S(2)}) collective-permute-start(bf16[4,4,16,512]{3,2,1,0:T(8,128)(2,1)S(1)} %get-tuple-element.36), channel_id=1, source_target_pairs={{0,2},{1,3},{2,0},{3,1},{4,6},{5,7},{6,4},{7,5},{8,10},{9,11},{10,... | collective-permute-start | bytes 786440 | tf_op jit(solution)/shard_map/ppermute | solution.py:252
  19.1 1.5 %collective-permute-start.5 = (bf16[4,4,16,512]{3,2,1,0:T(8,128)(2,1)S(1)}, bf16[4,4,16,512]{3,2,1,0:T(8,128)(2,1)S(1)}, u32[]{:S(2)}, u32[]{:S(2)}) collective-permute-start(bf16[4,4,16,512]{3,2,1,0:T(8,128)(2,1)S(1)} %get-tuple-element.43), channel_id=1, source_target_pairs={{0,1},{1,0},{2,3},{3,2},{4,5},{5,4},{6,7},{7,6},{8,9},{9,8},{10,11... | collective-permute-start | bytes 786440 | tf_op jit(solution)/shard_map/ppermute | solution.py:252
  20.6 0.5 %collective-permute-start.4 = (bf16[4,4,16,512]{3,2,1,0:T(8,128)(2,1)S(1)}, bf16[4,4,16,512]{3,2,1,0:T(8,128)(2,1)S(1)}, u32[]{:S(2)}, u32[]{:S(2)}) collective-permute-start(bf16[4,4,16,512]{3,2,1,0:T(8,128)(2,1)S(1)} %get-tuple-element.42), channel_id=1, source_target_pairs={{0,3},{1,2},{2,1},{3,0},{4,7},{5,6},{6,5},{7,4},{8,11},{9,10},{10,... | collective-permute-start | bytes 786440 | tf_op jit(solution)/shard_map/ppermute | solution.py:252
  21.1 2.0 %rules_first.1 = (f32[2,1024,128]{2,1,0:T(8,128)S(1)}, f32[2,200,1024]{2,1,0:T(8,128)S(1)}) custom-call(bf16[4,4,16,512]{3,2,1,0:T(8,128)(2,1)S(1)} %get-tuple-element.28.refs_0_, bf16[4,4,16,512]{3,2,1,0:T(8,128)(2,1)S(1)} %collective-permute-done.refs_1_, ...), custom_call_target="tpu_custom_call", output_to_operand_aliasing={{0}: (8, {}), {1}: (9, {})} | custom-call | tf_op jit(solution)/shard_map/rules_first/pallas_call | solution.py:214
  23.1 0.9 %collective-permute-done.3.refs_0_ = bf16[4,4,16,512]{3,2,1,0:T(8,128)(2,1)S(1)} collective-permute-done((bf16[4,4,16,512]{3,2,1,0:T(8,128)(2,1)S(1)}, bf16[4,4,16,512]{3,2,1,0:T(8,128)(2,1)S(1)}, u32[]{:S(2)}, u32[]{:S(2)}) %collective-permute-start.3) | collective-permute-done | bytes 262176 | tf_op jit(solution)/shard_map/ppermute | solution.py:252
  24.0 2.1 %rules_gather.1 = (f32[2,1024,128]{2,1,0:T(8,128)S(1)}, f32[2,200,1024]{2,1,0:T(8,128)S(1)}) custom-call(bf16[4,4,16,512]{3,2,1,0:T(8,128)(2,1)S(1)} %collective-permute-done.3.refs_0_, bf16[512,2048]{1,0:T(8,128)(2,1)S(1)} %get-tuple-element.32.refs_4_.refs_1_.refs_2_, ...), custom_call_target="tpu_custom_call", output_to_operand_aliasing={{0}: (5, {}), {1}: (6, {})} | custom-call | tf_op jit(solution)/shard_map/rules_gather/pallas_call | solution.py:214
  26.1 1.1 %rules_middle.1 = (f32[2,1024,128]{2,1,0:T(8,128)S(1)}, bf16[512,2048]{1,0:T(8,128)(2,1)S(1)}, bf16[512,200]{1,0:T(8,128)(2,1)S(1)}) custom-call(bf16[4,4,16,512]{3,2,1,0:T(8,128)(2,1)S(1)} %collective-permute-done.5.refs_0_, bf16[512,2048]{1,0:T(8,128)(2,1)S(1)} %get-tuple-element.32.refs_4_.refs_1_.refs_2_, ...), custom_call_target="tpu_custom_call", output_to_operand_aliasing={{0}: (5, {})} | custom-call | tf_op jit(solution)/shard_map/rules_middle/pallas_call | solution.py:214
  27.3 1.0 %collective-permute-done.4.refs_1_ = bf16[4,4,16,512]{3,2,1,0:T(8,128)(2,1)S(1)} collective-permute-done((bf16[4,4,16,512]{3,2,1,0:T(8,128)(2,1)S(1)}, bf16[4,4,16,512]{3,2,1,0:T(8,128)(2,1)S(1)}, u32[]{:S(2)}, u32[]{:S(2)}) %collective-permute-start.4) | collective-permute-done | bytes 262176 | tf_op jit(solution)/shard_map/ppermute | solution.py:252
  28.3 1.9 %rules_last.1 = (bf16[1,200,1024]{2,1,0:T(8,128)(2,1)S(1)}, f32[2,1024,128]{2,1,0:T(8,128)S(1)}, bf16[512,2048]{1,0:T(8,128)(2,1)S(1)}, bf16[512,200]{1,0:T(8,128)(2,1)S(1)}) custom-call(f32[2,200,1024]{2,1,0:T(8,128)S(1)} %get-tuple-element.41.refs_0_.acc_ref, ...), custom_call_target="tpu_custom_call", output_to_operand_aliasing={{1}: (6, {}), {2}: (7, {}), {3}: (8, {})} | custom-call | tf_op jit(solution)/shard_map/rules_last/pallas_call | solution.py:214
  30.2 1.2 %collective-permute-start.6 = (bf16[200,1024]{1,0:T(8,128)(2,1)S(1)}, bf16[200,1024]{1,0:T(8,128)(2,1)S(1)}, u32[]{:S(2)}, u32[]{:S(2)}) collective-permute-start(bf16[200,1024]{1,0:T(8,128)(2,1)S(1)} %bitcast.12), channel_id=1, source_target_pairs={{0,16},{16,0},{1,17},{17,1},{2,18},{18,2},{3,19},{19,3},{4,20},{20... | collective-permute-start | bytes 1228808 | tf_op jit(solution)/shard_map/ppermute | solution.py:317
  31.4 1.6 %rules_finish.1 = (bf16[16,64,200]{2,1,0:T(8,128)(2,1)}, f32[200,1024]{1,0:T(8,128)S(1)}) custom-call(bf16[512,2048]{1,0:T(8,128)(2,1)S(1)} %get-tuple-element.48.feat, bf16[512,200]{1,0:T(8,128)(2,1)S(1)} %get-tuple-element.49.slope, f32[2,200,1024]{2,1,0:T(8,128)S(1)} %get-tuple-element.41.refs_0_.acc_ref, f32[2,1024,128]{2,1,0:T(8,128)S(1)} %get-tuple-element.50.disp_ref), custom_call_target="tpu_custom_call" | custom-call | tf_op jit(solution)/shard_map/rules_finish/pallas_call | solution.py:214
  32.9 1.0 %add.1 = f32[200,1024]{1,0:T(8,128)} custom-call(f32[200,1024]{1,0:T(8,128)S(1)} %get-tuple-element.52.own_ref, bf16[200,1024]{1,0:T(8,128)(2,1)S(1)} %collective-permute-done.6.refs_0_), custom_call_target="tpu_custom_call" | custom-call | tf_op jit(solution)/shard_map/add/pallas_call | solution.py:320
  (9 shorter events, 0.1 us)
Async XLA Ops:
  0.6 1.2 %copy-start.1 = (bf16[4,256,512]{2,1,0:T(8,128)(2,1)S(1)}, bf16[4,256,512]{2,1,0:T(8,128)(2,1)}, u32[]{:S(2)}) copy-start(bf16[4,256,512]{2,1,0:T(8,128)(2,1)} %param.5) | copy-start | bytes 3145732
  1.9 11.4 %collective-permute-start = (bf16[4,4,16,512]{3,2,1,0:T(8,128)(2,1)S(1)}, bf16[4,4,16,512]{3,2,1,0:T(8,128)(2,1)S(1)}, u32[]{:S(2)}, u32[]{:S(2)}) collective-permute-start(bf16[4,4,16,512]{3,2,1,0:T(8,128)(2,1)S(1)} %get-tuple-element.29), channel_id=1, source_target_pairs={{0,8},{1,9},{2,10},{3,11},{4,12},{5,13},{6,14},{7,15},{8,0},{9,1},... | collective-permute-start | bytes 786440 | tf_op jit(solution)/shard_map/ppermute | solution.py:252
  6.0 7.7 %collective-permute-start.1 = (bf16[4,4,16,512]{3,2,1,0:T(8,128)(2,1)S(1)}, bf16[4,4,16,512]{3,2,1,0:T(8,128)(2,1)S(1)}, u32[]{:S(2)}, u32[]{:S(2)}) collective-permute-start(bf16[4,4,16,512]{3,2,1,0:T(8,128)(2,1)S(1)} %get-tuple-element.30), channel_id=1, source_target_pairs={{0,4},{1,5},{2,6},{3,7},{4,0},{5,1},{6,2},{7,3},{8,12},{9,13},{10,... | collective-permute-start | bytes 786440 | tf_op jit(solution)/shard_map/ppermute | solution.py:252
  7.6 9.9 %collective-permute-start.2 = (bf16[4,4,16,512]{3,2,1,0:T(8,128)(2,1)S(1)}, bf16[4,4,16,512]{3,2,1,0:T(8,128)(2,1)S(1)}, u32[]{:S(2)}, u32[]{:S(2)}) collective-permute-start(bf16[4,4,16,512]{3,2,1,0:T(8,128)(2,1)S(1)} %get-tuple-element.31), channel_id=1, source_target_pairs={{0,12},{1,13},{2,14},{3,15},{4,8},{5,9},{6,10},{7,11},{8,4},{9,5},... | collective-permute-start | bytes 786440 | tf_op jit(solution)/shard_map/ppermute | solution.py:252
  7.6 1.6 %copy-start = (bf16[512,2048]{1,0:T(8,128)(2,1)S(1)}, bf16[512,2048]{1,0:T(8,128)(2,1)}, u32[]{:S(2)}) copy-start(bf16[512,2048]{1,0:T(8,128)(2,1)} %refs_0_.1) | copy-start | bytes 6291460
  9.2 1.1 %copy-start.2 = (bf16[1,2048,200]{1,2,0:T(8,128)(2,1)S(1)}, bf16[1,2048,200]{1,2,0:T(8,128)(2,1)}, u32[]{:S(2)}) copy-start(bf16[1,2048,200]{1,2,0:T(8,128)(2,1)} %param.8) | copy-start | bytes 2457604
  10.3 0.9 %copy-start.3 = (bf16[512,200]{0,1:T(8,128)(2,1)S(1)}, bf16[512,200]{0,1:T(8,128)(2,1)}, u32[]{:S(2)}) copy-start(bf16[512,200]{0,1:T(8,128)(2,1)} %param.7) | copy-start | bytes 614404
  11.3 0.7 %copy-start.4 = (f32[1,200]{1,0:T(1,128)S(1)}, f32[1,200]{1,0:T(1,128)}, u32[]{:S(2)}) copy-start(f32[1,200]{1,0:T(1,128)} %refs_3_.1) | copy-start | bytes 2404
  17.6 6.4 %collective-permute-start.3 = (bf16[4,4,16,512]{3,2,1,0:T(8,128)(2,1)S(1)}, bf16[4,4,16,512]{3,2,1,0:T(8,128)(2,1)S(1)}, u32[]{:S(2)}, u32[]{:S(2)}) collective-permute-start(bf16[4,4,16,512]{3,2,1,0:T(8,128)(2,1)S(1)} %get-tuple-element.36), channel_id=1, source_target_pairs={{0,2},{1,3},{2,0},{3,1},{4,6},{5,7},{6,4},{7,5},{8,10},{9,11},{10,... | collective-permute-start | bytes 786440 | tf_op jit(solution)/shard_map/ppermute | solution.py:252
  19.1 7.0 %collective-permute-start.5 = (bf16[4,4,16,512]{3,2,1,0:T(8,128)(2,1)S(1)}, bf16[4,4,16,512]{3,2,1,0:T(8,128)(2,1)S(1)}, u32[]{:S(2)}, u32[]{:S(2)}) collective-permute-start(bf16[4,4,16,512]{3,2,1,0:T(8,128)(2,1)S(1)} %get-tuple-element.43), channel_id=1, source_target_pairs={{0,1},{1,0},{2,3},{3,2},{4,5},{5,4},{6,7},{7,6},{8,9},{9,8},{10,11... | collective-permute-start | bytes 786440 | tf_op jit(solution)/shard_map/ppermute | solution.py:252
  20.6 7.6 %collective-permute-start.4 = (bf16[4,4,16,512]{3,2,1,0:T(8,128)(2,1)S(1)}, bf16[4,4,16,512]{3,2,1,0:T(8,128)(2,1)S(1)}, u32[]{:S(2)}, u32[]{:S(2)}) collective-permute-start(bf16[4,4,16,512]{3,2,1,0:T(8,128)(2,1)S(1)} %get-tuple-element.42), channel_id=1, source_target_pairs={{0,3},{1,2},{2,1},{3,0},{4,7},{5,6},{6,5},{7,4},{8,11},{9,10},{10,... | collective-permute-start | bytes 786440 | tf_op jit(solution)/shard_map/ppermute | solution.py:252
  30.2 2.7 %collective-permute-start.6 = (bf16[200,1024]{1,0:T(8,128)(2,1)S(1)}, bf16[200,1024]{1,0:T(8,128)(2,1)S(1)}, u32[]{:S(2)}, u32[]{:S(2)}) collective-permute-start(bf16[200,1024]{1,0:T(8,128)(2,1)S(1)} %bitcast.12), channel_id=1, source_target_pairs={{0,16},{16,0},{1,17},{17,1},{2,18},{18,2},{3,19},{19,3},{4,20},{20... | collective-permute-start | bytes 1228808 | tf_op jit(solution)/shard_map/ppermute | solution.py:317

commit v7 on v5

--- a/solution.py
+++ b/solution.py
@@ -176,11 +176,14 @@
 
 
 def last_kernel(cfg, ms, at, row_scale, *refs):
-    acc_ref, send_ref, refs = refs[0], refs[-4], refs[1:-4] + refs[-3:]
+    acc_ref, send_ref, part, refs = refs[0], refs[-5], refs[-1], refs[1:-5] + refs[-4:-1]
+    _, feat, slope = refs[-3:]
+    old, new = pl.ds(0, at), pl.ds(at, feat.shape[0] - at)
+    for i, cols, g in grad_parts(cfg[0], slope.at[old], feat.at[old], range(1, cfg[0])):
+        part[i, :, cols] = g + acc_ref[i, :, cols]
     middle_kernel(cfg, ms, at, *refs)
-    _, feat, slope = refs[-3:]
-    for i, cols, g in grad_parts(cfg[0], slope, feat, range(1, cfg[0])):
-        send_ref[i, :, cols] = ((g + acc_ref[i, :, cols]) * row_scale).astype(BF16)
+    for i, cols, g in grad_parts(cfg[0], slope.at[new], feat.at[new], range(1, cfg[0])):
+        send_ref[i, :, cols] = ((g + part[i, :, cols]) * row_scale).astype(BF16)
 
 
 def finish_kernel(groups, row_scale, feat, slope, acc_ref, disp_ref, dec_ref, own_ref):
@@ -288,7 +291,8 @@
     send, disp, feat, slope = call(
         functools.partial(last_kernel, cfg, last, at, row_scale), "rules_last",
         [bf(max(groups - 1, 1), regions, share), *shapes],
-        [acc, *inputs(last), *weights, *state], aliases={k + i: 1 + i for i in range(len(state))},
+        [acc, *inputs(last), *weights, *state],
+        [pltpu.VMEM((max(groups - 1, 1), regions, share), F32)], {k + i: 1 + i for i in range(len(state))},
     )
     decisions, grad = call(
         functools.partial(finish_kernel, groups, row_scale), "rules_finish",

time: 34.5 us -> 34.2 us (level)
  no operation moved by 1% of the time
where the time goes in v7:
time: 34.2 us; the launch traced here: 33.6 us
  starting transfers between devices  10.4 us (30%)
  Pallas kernels  8.71 us (25%)
  waiting for transfers between devices  7.24 us (21%)
  local copies, waits for them, and re-layouts  5.56 us (16%)
  other arithmetic  1.02 us (3%)
  between operations  0.69 us (2%)
    ppermute x6, starting transfers between devices, hop(): return lax.ppermute(x, ('grp', 'blk'), pairs)  9.23 us
    pallas_call x8, Pallas kernels, call(): pl.pallas_call(kernel, out_shape=tuple(outs), in_specs=[vmem] * len(opera...  8.71 us
    ppermute x6, waiting for transfers between devices, hop(): return lax.ppermute(x, ('grp', 'blk'), pairs)  7.24 us
    unnamed x10, local copies, waits for them, and re-layouts  5.56 us
    ppermute x1, starting transfers between devices, body(): grad = grad + lax.ppermute(send[step - 1], 'grp', pairs).astype(F32)  1.17 us
    broadcast_in_dim x1, other arithmetic, body(): return (decisions, grad.T[None])  1.02 us
  transfers between devices with their start and end apart: 7, of which 5 were waited for; matrix products, arithmetic and copies ran while one was open for 0% of the time, Pallas kernels for 21%

profile of v7, /device:TPU:0, one launch (start us, length us, event | category | flops | bytes accessed | tf_op | source)
XLA Modules:
  0.0 33.6 jit_solution(17725412975106810583)
XLA Ops:
  0.6 1.2 %copy-done.1 = bf16[4,256,512]{2,1,0:T(8,128)(2,1)S(1)} copy-done((bf16[4,256,512]{2,1,0:T(8,128)(2,1)S(1)}, bf16[4,256,512]{2,1,0:T(8,128)(2,1)}, u32[]{:S(2)}) %copy-start.1) | copy-done | bytes 1048600
  1.9 0.1 pack.1
  1.9 4.1 %collective-permute-start = (bf16[4,4,16,512]{3,2,1,0:T(8,128)(2,1)S(1)}, bf16[4,4,16,512]{3,2,1,0:T(8,128)(2,1)S(1)}, u32[]{:S(2)}, u32[]{:S(2)}) collective-permute-start(bf16[4,4,16,512]{3,2,1,0:T(8,128)(2,1)S(1)} %get-tuple-element.29), channel_id=1, source_target_pairs={{0,8},{1,9},{2,10},{3,11},{4,12},{5,13},{6,14},{7,15},{8,0},{9,1},... | collective-permute-start | bytes 786440 | tf_op jit(solution)/shard_map/ppermute | solution.py:238
  6.0 1.6 %collective-permute-start.1 = (bf16[4,4,16,512]{3,2,1,0:T(8,128)(2,1)S(1)}, bf16[4,4,16,512]{3,2,1,0:T(8,128)(2,1)S(1)}, u32[]{:S(2)}, u32[]{:S(2)}) collective-permute-start(bf16[4,4,16,512]{3,2,1,0:T(8,128)(2,1)S(1)} %get-tuple-element.30), channel_id=1, source_target_pairs={{0,4},{1,5},{2,6},{3,7},{4,0},{5,1},{6,2},{7,3},{8,12},{9,13},{10,... | collective-permute-start | bytes 786440 | tf_op jit(solution)/shard_map/ppermute | solution.py:238
  7.6 1.6 %copy-done = bf16[512,2048]{1,0:T(8,128)(2,1)S(1)} copy-done((bf16[512,2048]{1,0:T(8,128)(2,1)S(1)}, bf16[512,2048]{1,0:T(8,128)(2,1)}, u32[]{:S(2)}) %copy-start) | copy-done | bytes 2097176
  9.2 1.1 %copy-done.2 = bf16[1,2048,200]{1,2,0:T(8,128)(2,1)S(1)} copy-done((bf16[1,2048,200]{1,2,0:T(8,128)(2,1)S(1)}, bf16[1,2048,200]{1,2,0:T(8,128)(2,1)}, u32[]{:S(2)}) %copy-start.2) | copy-done | bytes 819224
  10.3 0.9 %copy-done.3 = bf16[512,200]{0,1:T(8,128)(2,1)S(1)} copy-done((bf16[512,200]{0,1:T(8,128)(2,1)S(1)}, bf16[512,200]{0,1:T(8,128)(2,1)}, u32[]{:S(2)}) %copy-start.3) | copy-done | bytes 204824
  11.3 0.7 %copy-done.4 = f32[1,200]{1,0:T(1,128)S(1)} copy-done((f32[1,200]{1,0:T(1,128)S(1)}, f32[1,200]{1,0:T(1,128)}, u32[]{:S(2)}) %copy-start.4) | copy-done | bytes 824
  12.0 0.2 load.1
  12.2 1.1 %collective-permute-done.refs_1_ = bf16[4,4,16,512]{3,2,1,0:T(8,128)(2,1)S(1)} collective-permute-done((bf16[4,4,16,512]{3,2,1,0:T(8,128)(2,1)S(1)}, bf16[4,4,16,512]{3,2,1,0:T(8,128)(2,1)S(1)}, u32[]{:S(2)}, u32[]{:S(2)}) %collective-permute-start) | collective-permute-done | bytes 262176 | tf_op jit(solution)/shard_map/ppermute | solution.py:238
  13.3 0.5 %collective-permute-done.1.refs_2_ = bf16[4,4,16,512]{3,2,1,0:T(8,128)(2,1)S(1)} collective-permute-done((bf16[4,4,16,512]{3,2,1,0:T(8,128)(2,1)S(1)}, bf16[4,4,16,512]{3,2,1,0:T(8,128)(2,1)S(1)}, u32[]{:S(2)}, u32[]{:S(2)}) %collective-permute-start.1) | collective-permute-done | bytes 262176 | tf_op jit(solution)/shard_map/ppermute | solution.py:238
  13.8 3.7 %collective-permute-done.2.refs_3_ = bf16[4,4,16,512]{3,2,1,0:T(8,128)(2,1)S(1)} collective-permute-done((bf16[4,4,16,512]{3,2,1,0:T(8,128)(2,1)S(1)}, bf16[4,4,16,512]{3,2,1,0:T(8,128)(2,1)S(1)}, u32[]{:S(2)}, u32[]{:S(2)}) %collective-permute-start.2) | collective-permute-done | bytes 262176 | tf_op jit(solution)/shard_map/ppermute | solution.py:238
  17.6 1.6 %collective-permute-start.3 = (bf16[4,4,16,512]{3,2,1,0:T(8,128)(2,1)S(1)}, bf16[4,4,16,512]{3,2,1,0:T(8,128)(2,1)S(1)}, u32[]{:S(2)}, u32[]{:S(2)}) collective-permute-start(bf16[4,4,16,512]{3,2,1,0:T(8,128)(2,1)S(1)} %get-tuple-element.36), channel_id=1, source_target_pairs={{0,2},{1,3},{2,0},{3,1},{4,6},{5,7},{6,4},{7,5},{8,10},{9,11},{10,... | collective-permute-start | bytes 786440 | tf_op jit(solution)/shard_map/ppermute | solution.py:238
  19.1 1.5 %collective-permute-start.5 = (bf16[4,4,16,512]{3,2,1,0:T(8,128)(2,1)S(1)}, bf16[4,4,16,512]{3,2,1,0:T(8,128)(2,1)S(1)}, u32[]{:S(2)}, u32[]{:S(2)}) collective-permute-start(bf16[4,4,16,512]{3,2,1,0:T(8,128)(2,1)S(1)} %get-tuple-element.43), channel_id=1, source_target_pairs={{0,1},{1,0},{2,3},{3,2},{4,5},{5,4},{6,7},{7,6},{8,9},{9,8},{10,11... | collective-permute-start | bytes 786440 | tf_op jit(solution)/shard_map/ppermute | solution.py:238
  20.6 0.5 %collective-permute-start.4 = (bf16[4,4,16,512]{3,2,1,0:T(8,128)(2,1)S(1)}, bf16[4,4,16,512]{3,2,1,0:T(8,128)(2,1)S(1)}, u32[]{:S(2)}, u32[]{:S(2)}) collective-permute-start(bf16[4,4,16,512]{3,2,1,0:T(8,128)(2,1)S(1)} %get-tuple-element.42), channel_id=1, source_target_pairs={{0,3},{1,2},{2,1},{3,0},{4,7},{5,6},{6,5},{7,4},{8,11},{9,10},{10,... | collective-permute-start | bytes 786440 | tf_op jit(solution)/shard_map/ppermute | solution.py:238
  21.1 2.0 %rules_first.1 = (f32[2,1024,128]{2,1,0:T(8,128)S(1)}, f32[2,200,1024]{2,1,0:T(8,128)S(1)}) custom-call(bf16[4,4,16,512]{3,2,1,0:T(8,128)(2,1)S(1)} %get-tuple-element.28.refs_0_, bf16[4,4,16,512]{3,2,1,0:T(8,128)(2,1)S(1)} %collective-permute-done.refs_1_, ...), custom_call_target="tpu_custom_call", output_to_operand_aliasing={{0}: (8, {}), {1}: (9, {})} | custom-call | tf_op jit(solution)/shard_map/rules_first/pallas_call | solution.py:200
  23.1 0.9 %collective-permute-done.3.refs_0_ = bf16[4,4,16,512]{3,2,1,0:T(8,128)(2,1)S(1)} collective-permute-done((bf16[4,4,16,512]{3,2,1,0:T(8,128)(2,1)S(1)}, bf16[4,4,16,512]{3,2,1,0:T(8,128)(2,1)S(1)}, u32[]{:S(2)}, u32[]{:S(2)}) %collective-permute-start.3) | collective-permute-done | bytes 262176 | tf_op jit(solution)/shard_map/ppermute | solution.py:238
  24.0 2.1 %rules_gather.1 = (f32[2,1024,128]{2,1,0:T(8,128)S(1)}, f32[2,200,1024]{2,1,0:T(8,128)S(1)}) custom-call(bf16[4,4,16,512]{3,2,1,0:T(8,128)(2,1)S(1)} %collective-permute-done.3.refs_0_, bf16[512,2048]{1,0:T(8,128)(2,1)S(1)} %get-tuple-element.32.refs_4_.refs_1_.refs_2_, ...), custom_call_target="tpu_custom_call", output_to_operand_aliasing={{0}: (5, {}), {1}: (6, {})} | custom-call | tf_op jit(solution)/shard_map/rules_gather/pallas_call | solution.py:200
  26.1 1.1 %rules_middle.1 = (f32[2,1024,128]{2,1,0:T(8,128)S(1)}, bf16[512,2048]{1,0:T(8,128)(2,1)S(1)}, bf16[512,200]{1,0:T(8,128)(2,1)S(1)}) custom-call(bf16[4,4,16,512]{3,2,1,0:T(8,128)(2,1)S(1)} %collective-permute-done.5.refs_0_, bf16[512,2048]{1,0:T(8,128)(2,1)S(1)} %get-tuple-element.32.refs_4_.refs_1_.refs_2_, ...), custom_call_target="tpu_custom_call", output_to_operand_aliasing={{0}: (5, {})} | custom-call | tf_op jit(solution)/shard_map/rules_middle/pallas_call | solution.py:200
  27.3 1.0 %collective-permute-done.4.refs_1_ = bf16[4,4,16,512]{3,2,1,0:T(8,128)(2,1)S(1)} collective-permute-done((bf16[4,4,16,512]{3,2,1,0:T(8,128)(2,1)S(1)}, bf16[4,4,16,512]{3,2,1,0:T(8,128)(2,1)S(1)}, u32[]{:S(2)}, u32[]{:S(2)}) %collective-permute-start.4) | collective-permute-done | bytes 262176 | tf_op jit(solution)/shard_map/ppermute | solution.py:238
  28.3 1.6 %rules_last.1 = (bf16[1,200,1024]{2,1,0:T(8,128)(2,1)S(1)}, f32[2,1024,128]{2,1,0:T(8,128)S(1)}, bf16[512,2048]{1,0:T(8,128)(2,1)S(1)}, bf16[512,200]{1,0:T(8,128)(2,1)S(1)}) custom-call(f32[2,200,1024]{2,1,0:T(8,128)S(1)} %get-tuple-element.41.refs_0_.acc_ref, ...), custom_call_target="tpu_custom_call", output_to_operand_aliasing={{1}: (6, {}), {2}: (7, {}), {3}: (8, {})} | custom-call | tf_op jit(solution)/shard_map/rules_last/pallas_call | solution.py:200
  29.9 1.2 %collective-permute-start.6 = (bf16[200,1024]{1,0:T(8,128)(2,1)S(1)}, bf16[200,1024]{1,0:T(8,128)(2,1)S(1)}, u32[]{:S(2)}, u32[]{:S(2)}) collective-permute-start(bf16[200,1024]{1,0:T(8,128)(2,1)S(1)} %bitcast.13), channel_id=1, source_target_pairs={{0,16},{16,0},{1,17},{17,1},{2,18},{18,2},{3,19},{19,3},{4,20},{20... | collective-permute-start | bytes 1228808 | tf_op jit(solution)/shard_map/ppermute | solution.py:303
  31.1 1.6 %rules_finish.1 = (bf16[16,64,200]{2,1,0:T(8,128)(2,1)}, f32[200,1024]{1,0:T(8,128)S(1)}) custom-call(bf16[512,2048]{1,0:T(8,128)(2,1)S(1)} %get-tuple-element.48.feat, bf16[512,200]{1,0:T(8,128)(2,1)S(1)} %get-tuple-element.49.slope, f32[2,200,1024]{2,1,0:T(8,128)S(1)} %get-tuple-element.41.refs_0_.acc_ref, f32[2,1024,128]{2,1,0:T(8,128)S(1)} %get-tuple-element.50.disp_ref), custom_call_target="tpu_custom_call" | custom-call | tf_op jit(solution)/shard_map/rules_finish/pallas_call | solution.py:200
  32.6 1.0 %add_bitcast_fusion = f32[1,1024,200]{1,2,0:T(8,128)} fusion(f32[200,1024]{1,0:T(8,128)S(1)} %get-tuple-element.52, bf16[200,1024]{1,0:T(8,128)(2,1)S(1)} %collective-permute-done.6), kind=kLoop, calls=%fused_computation | loop fusion | flops 409600 | bytes 2048000 | tf_op jit(solution)/shard_map/broadcast_in_dim | solution.py:304
  (9 shorter events, 0.1 us)
Async XLA Ops:
  0.6 1.2 %copy-start.1 = (bf16[4,256,512]{2,1,0:T(8,128)(2,1)S(1)}, bf16[4,256,512]{2,1,0:T(8,128)(2,1)}, u32[]{:S(2)}) copy-start(bf16[4,256,512]{2,1,0:T(8,128)(2,1)} %param.5) | copy-start | bytes 3145732
  1.9 11.4 %collective-permute-start = (bf16[4,4,16,512]{3,2,1,0:T(8,128)(2,1)S(1)}, bf16[4,4,16,512]{3,2,1,0:T(8,128)(2,1)S(1)}, u32[]{:S(2)}, u32[]{:S(2)}) collective-permute-start(bf16[4,4,16,512]{3,2,1,0:T(8,128)(2,1)S(1)} %get-tuple-element.29), channel_id=1, source_target_pairs={{0,8},{1,9},{2,10},{3,11},{4,12},{5,13},{6,14},{7,15},{8,0},{9,1},... | collective-permute-start | bytes 786440 | tf_op jit(solution)/shard_map/ppermute | solution.py:238
  6.0 7.7 %collective-permute-start.1 = (bf16[4,4,16,512]{3,2,1,0:T(8,128)(2,1)S(1)}, bf16[4,4,16,512]{3,2,1,0:T(8,128)(2,1)S(1)}, u32[]{:S(2)}, u32[]{:S(2)}) collective-permute-start(bf16[4,4,16,512]{3,2,1,0:T(8,128)(2,1)S(1)} %get-tuple-element.30), channel_id=1, source_target_pairs={{0,4},{1,5},{2,6},{3,7},{4,0},{5,1},{6,2},{7,3},{8,12},{9,13},{10,... | collective-permute-start | bytes 786440 | tf_op jit(solution)/shard_map/ppermute | solution.py:238
  7.6 9.9 %collective-permute-start.2 = (bf16[4,4,16,512]{3,2,1,0:T(8,128)(2,1)S(1)}, bf16[4,4,16,512]{3,2,1,0:T(8,128)(2,1)S(1)}, u32[]{:S(2)}, u32[]{:S(2)}) collective-permute-start(bf16[4,4,16,512]{3,2,1,0:T(8,128)(2,1)S(1)} %get-tuple-element.31), channel_id=1, source_target_pairs={{0,12},{1,13},{2,14},{3,15},{4,8},{5,9},{6,10},{7,11},{8,4},{9,5},... | collective-permute-start | bytes 786440 | tf_op jit(solution)/shard_map/ppermute | solution.py:238
  7.6 1.6 %copy-start = (bf16[512,2048]{1,0:T(8,128)(2,1)S(1)}, bf16[512,2048]{1,0:T(8,128)(2,1)}, u32[]{:S(2)}) copy-start(bf16[512,2048]{1,0:T(8,128)(2,1)} %refs_0_.1) | copy-start | bytes 6291460
  9.2 1.1 %copy-start.2 = (bf16[1,2048,200]{1,2,0:T(8,128)(2,1)S(1)}, bf16[1,2048,200]{1,2,0:T(8,128)(2,1)}, u32[]{:S(2)}) copy-start(bf16[1,2048,200]{1,2,0:T(8,128)(2,1)} %param.8) | copy-start | bytes 2457604
  10.3 0.9 %copy-start.3 = (bf16[512,200]{0,1:T(8,128)(2,1)S(1)}, bf16[512,200]{0,1:T(8,128)(2,1)}, u32[]{:S(2)}) copy-start(bf16[512,200]{0,1:T(8,128)(2,1)} %param.7) | copy-start | bytes 614404
  11.3 0.7 %copy-start.4 = (f32[1,200]{1,0:T(1,128)S(1)}, f32[1,200]{1,0:T(1,128)}, u32[]{:S(2)}) copy-start(f32[1,200]{1,0:T(1,128)} %refs_3_.1) | copy-start | bytes 2404
  17.6 6.4 %collective-permute-start.3 = (bf16[4,4,16,512]{3,2,1,0:T(8,128)(2,1)S(1)}, bf16[4,4,16,512]{3,2,1,0:T(8,128)(2,1)S(1)}, u32[]{:S(2)}, u32[]{:S(2)}) collective-permute-start(bf16[4,4,16,512]{3,2,1,0:T(8,128)(2,1)S(1)} %get-tuple-element.36), channel_id=1, source_target_pairs={{0,2},{1,3},{2,0},{3,1},{4,6},{5,7},{6,4},{7,5},{8,10},{9,11},{10,... | collective-permute-start | bytes 786440 | tf_op jit(solution)/shard_map/ppermute | solution.py:238
  19.1 7.0 %collective-permute-start.5 = (bf16[4,4,16,512]{3,2,1,0:T(8,128)(2,1)S(1)}, bf16[4,4,16,512]{3,2,1,0:T(8,128)(2,1)S(1)}, u32[]{:S(2)}, u32[]{:S(2)}) collective-permute-start(bf16[4,4,16,512]{3,2,1,0:T(8,128)(2,1)S(1)} %get-tuple-element.43), channel_id=1, source_target_pairs={{0,1},{1,0},{2,3},{3,2},{4,5},{5,4},{6,7},{7,6},{8,9},{9,8},{10,11... | collective-permute-start | bytes 786440 | tf_op jit(solution)/shard_map/ppermute | solution.py:238
  20.6 7.6 %collective-permute-start.4 = (bf16[4,4,16,512]{3,2,1,0:T(8,128)(2,1)S(1)}, bf16[4,4,16,512]{3,2,1,0:T(8,128)(2,1)S(1)}, u32[]{:S(2)}, u32[]{:S(2)}) collective-permute-start(bf16[4,4,16,512]{3,2,1,0:T(8,128)(2,1)S(1)} %get-tuple-element.42), channel_id=1, source_target_pairs={{0,3},{1,2},{2,1},{3,0},{4,7},{5,6},{6,5},{7,4},{8,11},{9,10},{10,... | collective-permute-start | bytes 786440 | tf_op jit(solution)/shard_map/ppermute | solution.py:238
  29.9 2.7 %collective-permute-start.6 = (bf16[200,1024]{1,0:T(8,128)(2,1)S(1)}, bf16[200,1024]{1,0:T(8,128)(2,1)S(1)}, u32[]{:S(2)}, u32[]{:S(2)}) collective-permute-start(bf16[200,1024]{1,0:T(8,128)(2,1)S(1)} %bitcast.13), channel_id=1, source_target_pairs={{0,16},{16,0},{1,17},{17,1},{2,18},{18,2},{3,19},{19,3},{4,20},{20... | collective-permute-start | bytes 1228808 | tf_op jit(solution)/shard_map/ppermute | solution.py:303
